TPU v7x, 512 devices: a whole 4x4x16 slice. The times are simulated.
512 devices in a mesh: tm: 128 (over z, y, core), chan: 4 (over x).
Axes of the slice: x: 4, y: 4, z: 16, core: 2. Of those that a mesh axis runs over, the one named last changes fastest.
Arguments:
- video: bfloat16 [512, 128, 512], P('tm', 'chan'), may hold values from -6 to 6
- clip_start: int32 [512], P('tm'), may hold values from 0 to 511, as said below
- first_conv_weight: bfloat16 [3, 128, 256], P(None, None, 'chan'), may hold values from -0.3125 to 0.3125
- second_conv_weight: bfloat16 [3, 256, 512], P(None, None, 'chan'), may hold values from -0.21875 to 0.21875
- cotangent: bfloat16 [256, 512, 512], P('tm', 'chan'), may hold values from -6 to 6
Outputs:
- encoded: bfloat16 [256, 512, 512], P('tm', 'chan')
- first_weight_gradient: float32 [3, 128, 256], P(None, None, 'chan')
- second_weight_gradient: float32 [3, 256, 512], P(None, None, 'chan')
Inputs may be any that keep to these rules, and one draw needn't show every extreme that they name: clip_start[0] = 0, clip_start[t] <= t, it never falls, and clip_start[clip_start[t]] = clip_start[t]; the last frame starts a clip of its own; clips have mixed lengths.
All inputs are finite; a program needn't handle non-finite values.
Results may differ from a plain program's by a relative error of at most 0.0049.
Values may be sent and summed in bfloat16 or wider, within the bound.
A program may use at most 64 MiB of HBM per device.

v0:
```python
import jax
import jax.numpy as jnp
from jax import lax
from jax.sharding import PartitionSpec as P


def passed_along(block, axis, distance):
    devices = range(lax.axis_size(axis))
    route = [(i - distance, i) for i in devices if i - distance in devices]
    return lax.ppermute(block, axis, route)


def per_device(video, clip_start, first_conv_weight, second_conv_weight, cotangent):
    frames = video.shape[0]
    halved = frames // 2
    positions = video.shape[2]
    my_index = lax.axis_index("tm")
    tap_offsets = jnp.arange(3, dtype=jnp.int32)
    frame_global = my_index * frames + jnp.arange(frames, dtype=jnp.int32)
    first_source = (
        jnp.maximum(frame_global[:, None] - tap_offsets[None, :], clip_start[:, None])
        - my_index * frames
        + 2
    )
    full_input = lax.all_gather(video, "chan", axis=1, tiled=True)
    earlier_input = passed_along(full_input[frames - 2 :], "tm", 1)
    input_ext = jnp.concatenate([earlier_input, full_input], axis=0)
    pre_activation = jnp.zeros((frames, first_conv_weight.shape[2], positions), jnp.float32)
    for filter_tap in range(3):
        selected_frames = jnp.take(input_ext, first_source[:, filter_tap], axis=0)
        pre_activation = pre_activation + jnp.einsum(
            "em,reu->rmu",
            first_conv_weight[filter_tap],
            selected_frames,
            preferred_element_type=jnp.float32,
        )
    sigmoid_pre = jax.nn.sigmoid(pre_activation)
    activated = pre_activation * sigmoid_pre
    downsampled = (0.5 * (activated[0::2] + activated[1::2])).astype(jnp.bfloat16)
    half_global = my_index * halved + jnp.arange(halved, dtype=jnp.int32)
    start_two = clip_start[0::2] // 2
    second_source = (
        jnp.maximum(half_global[:, None] - tap_offsets[None, :], start_two[:, None])
        - my_index * halved
        + 2
    )
    full_middle = lax.all_gather(downsampled, "chan", axis=1, tiled=True)
    earlier_middle = passed_along(full_middle, "tm", 1)
    middle_ext = jnp.concatenate([earlier_middle, full_middle], axis=0)
    encoded = jnp.zeros((halved, second_conv_weight.shape[2], positions), jnp.float32)
    for filter_tap in range(3):
        selected_frames = jnp.take(middle_ext, second_source[:, filter_tap], axis=0)
        encoded = encoded + jnp.einsum(
            "em,reu->rmu",
            second_conv_weight[filter_tap],
            selected_frames,
            preferred_element_type=jnp.float32,
        )
    encoded = encoded.astype(jnp.bfloat16)
    target_rows = jnp.arange(halved + 2, dtype=jnp.int32)
    gathered_terms = jnp.zeros((halved + 2, second_conv_weight.shape[1], positions), jnp.float32)
    for filter_tap in range(3):
        tap_contribution = jnp.einsum(
            "jk,dkp->djp",
            second_conv_weight[filter_tap],
            cotangent,
            preferred_element_type=jnp.float32,
        )
        selector = (target_rows[:, None] == second_source[:, filter_tap][None, :]).astype(
            jnp.float32
        )
        gathered_terms = gathered_terms + jnp.einsum(
            "ij,jcs->ics", selector, tap_contribution, precision=lax.Precision.HIGHEST
        )
    spilled = passed_along(gathered_terms[:2], "tm", -1)
    local_terms = gathered_terms[2:].at[halved - 2 :].add(spilled)
    unit_grads = lax.psum_scatter(local_terms, "chan", scatter_dimension=1, tiled=True)
    delta = (
        0.5
        * jnp.repeat(unit_grads, 2, axis=0)
        * sigmoid_pre
        * (1.0 + pre_activation * (1.0 - sigmoid_pre))
    ).astype(jnp.bfloat16)
    total_frames = frames * lax.axis_size("tm")
    first_scale = (total_frames * positions) ** (-0.5)
    second_scale = (total_frames // 2 * positions) ** (-0.5)
    first_weight_gradient = (
        jnp.stack(
            [
                jnp.einsum(
                    "rdm,rym->dy",
                    jnp.take(input_ext, first_source[:, filter_tap], axis=0),
                    delta,
                    preferred_element_type=jnp.float32,
                )
                for filter_tap in range(3)
            ]
        )
        * first_scale
    )
    second_weight_gradient = (
        jnp.stack(
            [
                jnp.einsum(
                    "rdm,rym->dy",
                    jnp.take(middle_ext, second_source[:, filter_tap], axis=0),
                    cotangent,
                    preferred_element_type=jnp.float32,
                )
                for filter_tap in range(3)
            ]
        )
        * second_scale
    )
    first_weight_gradient, second_weight_gradient = lax.psum(
        (first_weight_gradient, second_weight_gradient), "tm"
    )
    return (encoded, first_weight_gradient, second_weight_gradient)


def solution(mesh):
    in_specs = (
        P("tm", "chan", None),
        P("tm"),
        P(None, None, "chan"),
        P(None, None, "chan"),
        P("tm", "chan", None),
    )
    out_specs = (P("tm", "chan", None), P(None, None, "chan"), P(None, None, "chan"))
    return jax.shard_map(
        per_device, mesh=mesh, in_specs=in_specs, out_specs=out_specs, check_vma=False
    )
```

profile of v0, /device:TPU:1, one launch (start us, length us, event | category | flops | bytes accessed | tf_op | source)
XLA Modules:
  0.0 454.4 jit_solution(13346680975811821349)
XLA Ops:
  7.2 0.0 copy-start
  7.2 0.0 copy-start.4
  7.2 0.0 reduce-scatter.2.cloned.1.call-start
  7.2 0.9 copy-done
  8.1 1.2 fusion.17
  9.3 1.2 fusion.20
  10.5 1.2 fusion.14
  11.6 0.0 copy-done.4
  11.6 0.1 slice.94
  11.8 1.3 copy.19
  13.1 0.6 copy.18
  13.7 0.6 copy.20
  14.3 3.8 fusion.5
  18.1 2.8 fusion.7
  20.8 2.8 fusion.3
  23.6 1.8 copy_add_fusion
  25.3 0.0 copy-start.2
  25.3 1.1 slice.117
  26.4 8.8 %collective-permute-start.2 = (f32[2,256,512]{2,1,0:T(8,128)}, f32[2,256,512]{2,1,0:T(8,128)}, u32[]{:S(2)}, u32[]{:S(2)}) collective-permute-start(f32[2,256,512]{2,1,0:T(8,128)} %slice.117), channel_id=1, source_target_pairs={{4,0},{8,4},{12,8},{16,12},{20,16},{24,20},{28,24},{32,28},{36,32}... | collective-permute-start | bytes 3145736 | tf_op jit(solution)/shard_map/ppermute | solution.py:10
  35.2 0.0 copy-done.2
  35.2 11.6 %all_gather.6 = bf16[4,128,512]{2,1,0:T(8,128)(2,1)S(1)} all-gather(bf16[4,32,512]{2,1,0:T(8,128)(2,1)S(1)} %copy-done.2), channel_id=1, replica_groups=mesh['tm'=128,'chan'=4] {'chan'}, dimensions={1}, use_global_device_ids=true | all-gather | bytes 655360 | tf_op jit(solution)/shard_map/all_gather | solution.py:25
  46.8 1.9 collective-permute-start
  48.7 0.0 collective-permute-done.2
  48.8 2.4 slice_add_fusion
  51.2 0.0 reduce-scatter.2.cloned.1.call-update
  51.2 0.0 all-reduce.3.cloned.1.call-start
  51.4 0.6 collective-permute-done
  52.1 0.0 copy-start.3
  52.1 0.6 gather_fusion.1
  52.7 0.6 gather_fusion
  53.3 0.6 gather_fusion.2
  53.9 0.0 copy-done.3
  53.9 0.3 fusion.12
  54.2 0.3 convolution_add_fusion.1
  54.5 29.0 %reduce-scatter.2.cloned.1.call-done = f32[2,64,512]{2,1,0:T(8,128)} async-done(((f32[2,256,512]{2,1,0:T(8,128)}), f32[2,64,512]{2,1,0:T(8,128)}) %reduce-scatter.2.cloned.1.call-update) | async-done | bytes 262160 | tf_op jit(solution)/shard_map/reduce_scatter | solution.py:77
  83.6 1.0 broadcast_multiply_fusion
  84.5 0.5 fusion.10
  85.1 11.3 %all_gather.7 = bf16[2,256,512]{2,1,0:T(8,128)(2,1)S(1)} all-gather(bf16[2,64,512]{2,1,0:T(8,128)(2,1)S(1)} %multiply_convert_fusion), channel_id=1, replica_groups=mesh['tm'=128,'chan'=4] {'chan'}, dimensions={1}, use_global_device_ids=true | all-gather | bytes 655360 | tf_op jit(solution)/shard_map/all_gather | solution.py:47
  96.3 7.1 %collective-permute-start.1 = (bf16[2,256,512]{2,1,0:T(8,128)(2,1)S(1)}, bf16[2,256,512]{2,1,0:T(8,128)(2,1)S(1)}, u32[]{:S(2)}, u32[]{:S(2)}) collective-permute-start(bf16[2,256,512]{2,1,0:T(8,128)(2,1)S(1)} %all_gather.7), channel_id=1, source_target_pairs={{0,4},{4,8},{8,12},{12,16},{16,20},{20,24},{24,28},{28,32},{32,36}... | collective-permute-start | bytes 1572872 | tf_op jit(solution)/shard_map/ppermute | solution.py:10
  103.5 0.4 convolution_bitcast_fusion.4
  103.9 0.4 convolution_bitcast_fusion.5
  104.3 0.4 convolution_bitcast_fusion.3
  104.6 0.7 maximum_multiply_fusion.1
  105.3 0.0 copy-start.1
  105.3 4.1 collective-permute-done.1
  109.5 0.6 gather_fusion.4
  110.1 0.3 convolution_bitcast_fusion.1
  110.4 0.0 copy-done.1
  110.4 0.4 fusion.13
  110.9 0.6 gather_fusion.5
  111.5 0.6 gather_fusion.3
  112.1 0.3 convolution_bitcast_fusion.2
  112.4 0.4 convolution_add_fusion.3
  112.8 0.3 convolution_bitcast_fusion
  113.2 0.8 maximum_multiply_fusion
  114.0 0.0 all-reduce.3.cloned.1.call-update
  114.0 0.4 fusion.2
  114.4 0.9 copy.14
  115.3 329.0 %all-reduce.3.cloned.1.call-done = (f32[3,128,64]{1,2,0:T(8,128)}, f32[3,256,128]{2,1,0:T(8,128)}) async-done(((f32[3,128,64]{1,2,0:T(8,128)}, f32[3,256,128]{2,1,0:T(8,128)}), (f32[3,128,64]{1,2,0:T(8,128)}, f32[3,256,128]{2,1,0:T(8,128)})) %all-reduce.3.cloned.1.call-update) | async-done | bytes 491536 | tf_op jit(solution)/shard_map/psum | solution.py:115
  444.3 1.5 copy.30
  445.8 1.8 copy.31
  (18 shorter events, 0.3 us)
Async XLA Ops:
  7.2 1.0 copy-start
  7.2 4.5 copy-start.4
  7.2 76.4 %reduce-scatter.2.cloned.1.call-start = ((), (), s32[]{:S(2)}) async-start(), calls=%async_computation.1 | async-start | bytes 1310720 | tf_op jit(solution)/shard_map/reduce_scatter | solution.py:77
  25.3 9.9 %copy-start.2 = (bf16[4,32,512]{2,1,0:T(8,128)(2,1)S(1)}, bf16[4,32,512]{2,1,0:T(8,128)(2,1)}, u32[]{:S(2)}) copy-start(bf16[4,32,512]{2,1,0:T(8,128)(2,1)} %param.13) | copy-start | bytes 393220
  26.4 22.3 %collective-permute-start.2 = (f32[2,256,512]{2,1,0:T(8,128)}, f32[2,256,512]{2,1,0:T(8,128)}, u32[]{:S(2)}, u32[]{:S(2)}) collective-permute-start(f32[2,256,512]{2,1,0:T(8,128)} %slice.117), channel_id=1, source_target_pairs={{4,0},{8,4},{12,8},{16,12},{20,16},{24,20},{28,24},{32,28},{36,32}... | collective-permute-start | bytes 3145736 | tf_op jit(solution)/shard_map/ppermute | solution.py:10
  46.8 5.2 %collective-permute-start = (bf16[2,128,512]{2,1,0:T(8,128)(2,1)S(1)}, bf16[2,128,512]{2,1,0:T(8,128)(2,1)S(1)}, u32[]{:S(2)}, u32[]{:S(2)}) collective-permute-start(bf16[2,128,512]{2,1,0:T(8,128)(2,1)S(1)} %slice.115), channel_id=1, source_target_pairs={{0,4},{4,8},{8,12},{12,16},{16,20},{20,24},{24,28},{28,32},{32,36}... | collective-permute-start | bytes 786440 | tf_op jit(solution)/shard_map/ppermute | solution.py:10
  51.2 393.1 %all-reduce.3.cloned.1.call-start = ((), (), s32[]{:S(2)}) async-start(), calls=%async_computation.2 | async-start | bytes 983040 | tf_op jit(solution)/shard_map/psum | solution.py:115
  52.1 1.8 copy-start.3
  96.3 13.1 %collective-permute-start.1 = (bf16[2,256,512]{2,1,0:T(8,128)(2,1)S(1)}, bf16[2,256,512]{2,1,0:T(8,128)(2,1)S(1)}, u32[]{:S(2)}, u32[]{:S(2)}) collective-permute-start(bf16[2,256,512]{2,1,0:T(8,128)(2,1)S(1)} %all_gather.7), channel_id=1, source_target_pairs={{0,4},{4,8},{8,12},{12,16},{16,20},{20,24},{24,28},{28,32},{32,36}... | collective-permute-start | bytes 1572872 | tf_op jit(solution)/shard_map/ppermute | solution.py:10
  105.3 5.1 %copy-start.1 = (bf16[3,256,128]{2,1,0:T(8,128)(2,1)S(1)}, bf16[3,256,128]{2,1,0:T(8,128)(2,1)}, u32[]{:S(2)}) copy-start(bf16[3,256,128]{2,1,0:T(8,128)(2,1)} %param.16) | copy-start | bytes 589828
Sparse Core Ops, SparseCore 0:
  51.3 32.1 reduce-scatter.1
  114.1 330.1 all-reduce.2
where the time goes:
time: 455 us; the launch traced here: 454 us
  waiting for transfers between devices  363 us (80%)
  blocking collectives  22.9 us (5%)
  starting transfers between devices  17.9 us (4%)
  matrix products  17.3 us (4%)
  between operations  14.4 us (3%)
  local copies, waits for them, and re-layouts  12.3 us (3%)
  other arithmetic  6.72 us (1%)
    psum x1, waiting for transfers between devices, per_device(): lax.psum((first_weight_gradient, second_weight_gradient), 'tm')  329 us
    reduce_scatter x1, waiting for transfers between devices, per_device(): lax.psum_scatter(local_terms, 'chan', scatter_dimension=1, tiled=True)  29 us
    ppermute x3, starting transfers between devices, passed_along(): return lax.ppermute(block, axis, route)  17.8 us
    all_gather x1, blocking collectives, per_device(): full_input = lax.all_gather(video, 'chan', axis=1, tiled=True)  11.6 us
    all_gather x1, blocking collectives, per_device(): full_middle = lax.all_gather(downsampled, 'chan', axis=1, tiled=True)  11.3 us
    dot_general x3, matrix products, per_device(): jnp.einsum('ij,jcs->ics', selector, tap_contribution, precision=lax.Preci...  9.28 us
  transfers between devices with their start and end apart: 5, of which 4 were waited for; matrix products, arithmetic and copies ran while one was open for 2% of the time, Pallas kernels for 0%

commit v1 on v0

--- a/solution.py
+++ b/solution.py
@@ -1,6 +1,8 @@
 import jax
 import jax.numpy as jnp
 from jax import lax
+from jax.experimental import pallas as pl
+from jax.experimental.pallas import tpu as pltpu
 from jax.sharding import PartitionSpec as P
 
 
@@ -8,6 +10,100 @@
     devices = range(lax.axis_size(axis))
     route = [(i - distance, i) for i in devices if i - distance in devices]
     return lax.ppermute(block, axis, route)
+
+
+MESH = pl.DeviceIdType.MESH
+NQ = 8
+NZ = 16
+
+
+def sum_kernel(p1_ref, p2_ref, o1_ref, o2_ref, part, send1, recv1, mine, recv2, gather, held, sa, ra, sb, rb, sc, rc, sd, rd):
+    me = lax.axis_index("tm")
+    chan = lax.axis_index("chan")
+    z, q = me // NQ, lax.rem(me, NQ)
+
+    def in_z(s):
+        return (z * NQ + lax.rem(q + s, NQ), chan)
+
+    def over_z(s):
+        return (lax.rem(z + s, NZ) * NQ + q, chan)
+
+    barrier = pltpu.get_barrier_semaphore()
+    for s in range(1, NQ):
+        pl.semaphore_signal(barrier, inc=1, device_id=in_z(s), device_id_type=MESH)
+    for s in range(1, NZ):
+        pl.semaphore_signal(barrier, inc=1, device_id=over_z(s), device_id_type=MESH)
+    for i in range(6):
+        part[i] = p2_ref[i * 128 : (i + 1) * 128, :]
+    part[6] = p1_ref[0:128, :]
+    part[7] = jnp.concatenate([p1_ref[128:192, :], jnp.zeros((64, 128), jnp.float32)], axis=0)
+    send1[...] = part[...].astype(jnp.bfloat16)
+    pl.semaphore_wait(barrier, NQ + NZ - 2)
+
+    def exchange(n, src, dst, ssem, rsem, device):
+        copies = []
+        for s in range(1, n):
+            copy = pltpu.make_async_remote_copy(
+                src_ref=src(s), dst_ref=dst(s), send_sem=ssem.at[s], recv_sem=rsem.at[s],
+                device_id=device(s), device_id_type=MESH,
+            )
+            copy.start()
+            copies.append(copy)
+        return copies
+
+    first = exchange(NQ, lambda s: send1.at[lax.rem(q + s, NQ)], lambda s: recv1.at[s], sa, ra, in_z)
+    total = part[q]
+    for s in range(1, NQ):
+        first[s - 1].wait_recv()
+        total = total + recv1[s].astype(jnp.float32)
+    mine[...] = total.reshape(NZ, 8, 128)
+    second = exchange(NZ, lambda s: mine.at[lax.rem(z + s, NZ)], lambda s: recv2.at[s], sb, rb, over_z)
+    total = mine[z]
+    for s in range(1, NZ):
+        second[s - 1].wait_recv()
+        total = total + recv2[s]
+    gather[z] = total
+    third = exchange(NZ, lambda s: gather.at[z], lambda s: gather.at[z], sc, rc, over_z)
+    for copy in third:
+        copy.wait_recv()
+    held[q] = gather[...].reshape(128, 128).astype(jnp.bfloat16)
+    fourth = exchange(NQ, lambda s: held.at[q], lambda s: held.at[q], sd, rd, in_z)
+    for copy in fourth:
+        copy.wait_recv()
+    for k in range(3):
+        o2_ref[k] = held[2 * k : 2 * k + 2].reshape(256, 128).astype(jnp.float32) * (131072.0 ** -0.5)
+        piece = held[6 + k // 2, (k % 2) * 64 : (k % 2) * 64 + 64, :]
+        o1_ref[k] = piece.astype(jnp.float32).T * (262144.0 ** -0.5)
+    for copy in first + second + third + fourth:
+        copy.wait_send()
+
+
+def sum_over_frames(p1, p2):
+    vmem = pl.BlockSpec(memory_space=pltpu.VMEM)
+    dma = pltpu.SemaphoreType.DMA
+    return pl.pallas_call(
+        sum_kernel,
+        out_shape=(
+            jax.ShapeDtypeStruct((3, 128, 64), jnp.float32),
+            jax.ShapeDtypeStruct((3, 256, 128), jnp.float32),
+        ),
+        in_specs=[vmem] * 2,
+        out_specs=(vmem, vmem),
+        scratch_shapes=[
+            pltpu.VMEM((NQ, 128, 128), jnp.float32),
+            pltpu.VMEM((NQ, 128, 128), jnp.bfloat16),
+            pltpu.VMEM((NQ, 128, 128), jnp.bfloat16),
+            pltpu.VMEM((NZ, 8, 128), jnp.float32),
+            pltpu.VMEM((NZ, 8, 128), jnp.float32),
+            pltpu.VMEM((NZ, 8, 128), jnp.float32),
+            pltpu.VMEM((NQ, 128, 128), jnp.bfloat16),
+            dma((NQ,)), dma((NQ,)), dma((NZ,)), dma((NZ,)),
+            dma((NZ,)), dma((NZ,)), dma((NQ,)), dma((NQ,)),
+        ],
+        compiler_params=pltpu.CompilerParams(
+            collective_id=0, has_side_effects=True, vmem_limit_bytes=24 * 1024 * 1024
+        ),
+    )(p1, p2)
 
 
 def per_device(video, clip_start, first_conv_weight, second_conv_weight, cotangent):
@@ -81,14 +177,11 @@
         * sigmoid_pre
         * (1.0 + pre_activation * (1.0 - sigmoid_pre))
     ).astype(jnp.bfloat16)
-    total_frames = frames * lax.axis_size("tm")
-    first_scale = (total_frames * positions) ** (-0.5)
-    second_scale = (total_frames // 2 * positions) ** (-0.5)
     first_weight_gradient = (
         jnp.stack(
             [
                 jnp.einsum(
-                    "rdm,rym->dy",
+                    "rdm,rym->yd",
                     jnp.take(input_ext, first_source[:, filter_tap], axis=0),
                     delta,
                     preferred_element_type=jnp.float32,
@@ -96,7 +189,6 @@
                 for filter_tap in range(3)
             ]
         )
-        * first_scale
     )
     second_weight_gradient = (
         jnp.stack(
@@ -110,10 +202,9 @@
                 for filter_tap in range(3)
             ]
         )
-        * second_scale
-    )
-    first_weight_gradient, second_weight_gradient = lax.psum(
-        (first_weight_gradient, second_weight_gradient), "tm"
+    )
+    first_weight_gradient, second_weight_gradient = sum_over_frames(
+        first_weight_gradient.reshape(192, 128), second_weight_gradient.reshape(768, 128)
     )
     return (encoded, first_weight_gradient, second_weight_gradient)
 

time: 455 us -> 167 us (0.37)
  waiting for transfers between devices: 363 us -> 34.2 us
  Pallas kernels: 0 us -> 43.8 us
    psum x1 -> x0, waiting for transfers between devices: 329 us -> none  [per_device(): lax.psum((first_weight_gradient, second_weight_gradient), 'tm')]
    pallas_call x0 -> x1, Pallas kernels: none -> 43.8 us  [sum_over_frames(): pl.pallas_call(sum_kernel, out_shape=(jax.ShapeDtypeStruct((3, 128, 64),...]
  transfers between devices with their start and end apart: 5 -> 4, of which waited for: 4 -> 3; matrix products, arithmetic and copies ran while one was open for 2% -> 4% of each run, Pallas kernels for 0% -> 0%
where the time goes in v1:
time: 167 us
  Pallas kernels  43.8 us (26%)
  waiting for transfers between devices  34.2 us (20%)
  blocking collectives  22.9 us (14%)
  starting transfers between devices  18.2 us (11%)
  matrix products  17.3 us (10%)
  between operations  14.4 us (9%)
  local copies, waits for them, and re-layouts  10.5 us (6%)
  other arithmetic  5.32 us (3%)
    pallas_call x1, Pallas kernels, sum_over_frames(): pl.pallas_call(sum_kernel, out_shape=(jax.ShapeDtypeStruct((3, 128, 64),...  43.8 us
    reduce_scatter x1, waiting for transfers between devices, per_device(): lax.psum_scatter(local_terms, 'chan', scatter_dimension=1, tiled=True)  28.7 us
    ppermute x3, starting transfers between devices, passed_along(): return lax.ppermute(block, axis, route)  18.2 us
    all_gather x1, blocking collectives, per_device(): full_input = lax.all_gather(video, 'chan', axis=1, tiled=True)  11.6 us
    all_gather x1, blocking collectives, per_device(): full_middle = lax.all_gather(downsampled, 'chan', axis=1, tiled=True)  11.3 us
    dot_general x3, matrix products, per_device(): jnp.einsum('ij,jcs->ics', selector, tap_contribution, precision=lax.Preci...  9.28 us
    ppermute x3, waiting for transfers between devices, passed_along(): return lax.ppermute(block, axis, route)  5.44 us
    dot_general x3, matrix products, per_device(): jnp.einsum('jk,dkp->djp', second_conv_weight[filter_tap], cotangent, pref...  3.49 us
  transfers between devices with their start and end apart: 4, of which 3 were waited for; matrix products, arithmetic and copies ran while one was open for 4% of the time, Pallas kernels for 0%

profile of v1, /device:TPU:1, one launch (start us, length us, event | category | flops | bytes accessed | tf_op | source)
XLA Modules:
  0.0 166.7 jit_solution(14784427161382070974)
XLA Ops:
  7.2 0.0 copy-start
  7.2 0.0 copy-start.4
  7.2 0.0 reduce-scatter.2.cloned.1.call-start
  7.2 0.9 copy-done
  8.1 1.2 fusion.17
  9.3 1.2 fusion.20
  10.5 1.2 fusion.14
  11.6 0.0 copy-done.4
  11.6 0.1 slice.94
  11.8 1.3 copy.20
  13.1 0.6 copy.19
  13.7 0.6 copy.21
  14.3 3.8 %fusion.5 = f32[4,256,512]{2,0,1:T(4,128)S(1)} fusion(f32[2,512,256]{1,0,2:T(2,128)} %copy.20, s32[2]{0:T(128)S(1)} %get-tuple-element.48), kind=kOutput, calls=%fused_computation.24 | convolution fusion | flops 12582920 | bytes 3145736 | tf_op jit(solution)/shard_map/ij,jcs->ics/dot_general | solution.py:168
  18.0 2.8 %fusion.7 = f32[4,256,512]{2,0,1:T(4,128)S(1)} fusion(f32[2,512,256]{1,0,2:T(2,128)S(1)} %copy.19, s32[2]{0:T(128)S(1)} %get-tuple-element.46), kind=kOutput, calls=%fused_computation.26 | convolution fusion | flops 12582920 | bytes 3145736 | tf_op jit(solution)/shard_map/ij,jcs->ics/dot_general | solution.py:168
  20.8 2.8 %fusion.3 = f32[4,256,512]{2,0,1:T(4,128)S(1)} fusion(f32[2,512,256]{1,0,2:T(2,128)S(1)} %copy.21, s32[2]{0:T(128)S(1)} %get-tuple-element.47), kind=kOutput, calls=%fused_computation.22 | convolution fusion | flops 12582920 | bytes 3145736 | tf_op jit(solution)/shard_map/ij,jcs->ics/dot_general | solution.py:168
  23.6 1.8 %copy_add_fusion = f32[4,256,512]{2,1,0:T(8,128)S(1)} fusion(f32[4,256,512]{2,0,1:T(4,128)S(1)} %fusion.3, f32[4,256,512]{2,0,1:T(4,128)S(1)} %fusion.5, f32[4,256,512]{2,0,1:T(4,128)S(1)} %fusion.7), kind=kLoop, calls=%fused_computation.6 | loop fusion | flops 1048576 | bytes 8388608 | tf_op jit(solution)/shard_map/add | solution.py:168
  25.3 0.0 copy-start.2
  25.3 1.1 slice.117
  26.4 8.8 %collective-permute-start.2 = (f32[2,256,512]{2,1,0:T(8,128)}, f32[2,256,512]{2,1,0:T(8,128)}, u32[]{:S(2)}, u32[]{:S(2)}) collective-permute-start(f32[2,256,512]{2,1,0:T(8,128)} %slice.117), channel_id=1, source_target_pairs={{4,0},{8,4},{12,8},{16,12},{20,16},{24,20},{28,24},{32,28},{36,32}... | collective-permute-start | bytes 3145736 | tf_op jit(solution)/shard_map/ppermute | solution.py:12
  35.2 0.0 copy-done.2
  35.2 11.6 %all_gather.6 = bf16[4,128,512]{2,1,0:T(8,128)(2,1)S(1)} all-gather(bf16[4,32,512]{2,1,0:T(8,128)(2,1)S(1)} %copy-done.2), channel_id=1, replica_groups=mesh['tm'=128,'chan'=4] {'chan'}, dimensions={1}, use_global_device_ids=true | all-gather | bytes 655360 | tf_op jit(solution)/shard_map/all_gather | solution.py:121
  46.8 1.9 %collective-permute-start = (bf16[2,128,512]{2,1,0:T(8,128)(2,1)S(1)}, bf16[2,128,512]{2,1,0:T(8,128)(2,1)S(1)}, u32[]{:S(2)}, u32[]{:S(2)}) collective-permute-start(bf16[2,128,512]{2,1,0:T(8,128)(2,1)S(1)} %slice.115), channel_id=1, source_target_pairs={{0,4},{4,8},{8,12},{12,16},{16,20},{20,24},{24,28},{28,32},{32,36}... | collective-permute-start | bytes 786440 | tf_op jit(solution)/shard_map/ppermute | solution.py:12
  48.8 0.0 collective-permute-done.2
  48.8 2.4 %slice_add_fusion = f32[2,256,512]{2,1,0:T(8,128)} fusion(f32[2,256,512]{2,1,0:T(8,128)} %collective-permute-done.2, f32[4,256,512]{2,1,0:T(8,128)S(1)} %copy_add_fusion), kind=kLoop, calls=%fused_computation.21 | loop fusion | flops 262144 | bytes 3145728 | tf_op jit(solution)/shard_map/add | solution.py:172
  51.2 0.0 reduce-scatter.2.cloned.1.call-update
  51.4 0.7 collective-permute-done
  52.1 0.0 copy-start.3
  52.1 0.6 gather_fusion.1
  52.7 0.6 gather_fusion
  53.3 0.6 gather_fusion.2
  53.9 0.0 copy-done.3
  53.9 0.3 fusion.12
  54.2 0.3 convolution_add_fusion.1
  54.5 28.7 %reduce-scatter.2.cloned.1.call-done = f32[2,64,512]{2,1,0:T(8,128)} async-done(((f32[2,256,512]{2,1,0:T(8,128)}), f32[2,64,512]{2,1,0:T(8,128)}) %reduce-scatter.2.cloned.1.call-update) | async-done | bytes 262160 | tf_op jit(solution)/shard_map/reduce_scatter | solution.py:173
  83.2 1.0 broadcast_multiply_fusion
  84.2 0.5 fusion.10
  84.7 11.3 %all_gather.7 = bf16[2,256,512]{2,1,0:T(8,128)(2,1)S(1)} all-gather(bf16[2,64,512]{2,1,0:T(8,128)(2,1)S(1)} %multiply_convert_fusion), channel_id=1, replica_groups=mesh['tm'=128,'chan'=4] {'chan'}, dimensions={1}, use_global_device_ids=true | all-gather | bytes 655360 | tf_op jit(solution)/shard_map/all_gather | solution.py:143
  96.0 7.5 %collective-permute-start.1 = (bf16[2,256,512]{2,1,0:T(8,128)(2,1)S(1)}, bf16[2,256,512]{2,1,0:T(8,128)(2,1)S(1)}, u32[]{:S(2)}, u32[]{:S(2)}) collective-permute-start(bf16[2,256,512]{2,1,0:T(8,128)(2,1)S(1)} %all_gather.7), channel_id=1, source_target_pairs={{0,4},{4,8},{8,12},{12,16},{16,20},{20,24},{24,28},{28,32},{32,36}... | collective-permute-start | bytes 1572872 | tf_op jit(solution)/shard_map/ppermute | solution.py:12
  103.5 0.4 convolution_bitcast_fusion.4
  103.9 0.4 convolution_bitcast_fusion.5
  104.3 0.4 convolution_bitcast_fusion.3
  104.7 0.0 copy-start.1
  104.7 4.7 %collective-permute-done.1 = bf16[2,256,512]{2,1,0:T(8,128)(2,1)S(1)} collective-permute-done((bf16[2,256,512]{2,1,0:T(8,128)(2,1)S(1)}, bf16[2,256,512]{2,1,0:T(8,128)(2,1)S(1)}, u32[]{:S(2)}, u32[]{:S(2)}) %collective-permute-start.1) | collective-permute-done | bytes 524320 | tf_op jit(solution)/shard_map/ppermute | solution.py:12
  109.5 0.6 gather_fusion.4
  110.1 0.3 convolution_bitcast_fusion.1
  110.4 0.0 copy-done.1
  110.5 0.4 fusion.13
  110.9 0.6 gather_fusion.5
  111.5 0.6 gather_fusion.3
  112.1 0.3 convolution_bitcast_fusion
  112.4 0.3 convolution_bitcast_fusion.2
  112.8 43.8 %shard_map.81 = (f32[3,128,64]{2,1,0:T(8,128)S(1)}, f32[3,256,128]{2,1,0:T(8,128)S(1)}) custom-call(f32[192,128]{1,0:T(8,128)S(1)} %bitcast.114, f32[768,128]{1,0:T(8,128)S(1)} %bitcast.113), custom_call_target="tpu_custom_call" | custom-call | tf_op jit(solution)/shard_map/pallas_call | solution.py:84
  156.6 0.8 copy.15
  157.4 0.4 convolution_add_fusion.3
  157.8 0.4 fusion.2
  158.3 0.9 copy.14
  159.1 0.7 copy.30
  (20 shorter events, 0.3 us)
Async XLA Ops:
  7.2 1.0 copy-start
  7.2 4.5 %copy-start.4 = (s32[4]{0:T(128)S(1)}, s32[4]{0:T(128)}, u32[]{:S(2)}) copy-start(s32[4]{0:T(128)} %param.14) | copy-start | bytes 52
  7.2 76.1 %reduce-scatter.2.cloned.1.call-start = ((), (), s32[]{:S(2)}) async-start(), calls=%async_computation.1 | async-start | bytes 1310720 | tf_op jit(solution)/shard_map/reduce_scatter | solution.py:173
  25.3 9.9 %copy-start.2 = (bf16[4,32,512]{2,1,0:T(8,128)(2,1)S(1)}, bf16[4,32,512]{2,1,0:T(8,128)(2,1)}, u32[]{:S(2)}) copy-start(bf16[4,32,512]{2,1,0:T(8,128)(2,1)} %param.13) | copy-start | bytes 393220
  26.4 22.3 %collective-permute-start.2 = (f32[2,256,512]{2,1,0:T(8,128)}, f32[2,256,512]{2,1,0:T(8,128)}, u32[]{:S(2)}, u32[]{:S(2)}) collective-permute-start(f32[2,256,512]{2,1,0:T(8,128)} %slice.117), channel_id=1, source_target_pairs={{4,0},{8,4},{12,8},{16,12},{20,16},{24,20},{28,24},{32,28},{36,32}... | collective-permute-start | bytes 3145736 | tf_op jit(solution)/shard_map/ppermute | solution.py:12
  46.8 5.2 %collective-permute-start = (bf16[2,128,512]{2,1,0:T(8,128)(2,1)S(1)}, bf16[2,128,512]{2,1,0:T(8,128)(2,1)S(1)}, u32[]{:S(2)}, u32[]{:S(2)}) collective-permute-start(bf16[2,128,512]{2,1,0:T(8,128)(2,1)S(1)} %slice.115), channel_id=1, source_target_pairs={{0,4},{4,8},{8,12},{12,16},{16,20},{20,24},{24,28},{28,32},{32,36}... | collective-permute-start | bytes 786440 | tf_op jit(solution)/shard_map/ppermute | solution.py:12
  52.1 1.8 %copy-start.3 = (bf16[3,128,64]{1,2,0:T(8,128)(2,1)S(1)}, bf16[3,128,64]{1,2,0:T(8,128)(2,1)}, u32[]{:S(2)}) copy-start(bf16[3,128,64]{1,2,0:T(8,128)(2,1)} %param.15) | copy-start | bytes 147460
  96.0 13.4 %collective-permute-start.1 = (bf16[2,256,512]{2,1,0:T(8,128)(2,1)S(1)}, bf16[2,256,512]{2,1,0:T(8,128)(2,1)S(1)}, u32[]{:S(2)}, u32[]{:S(2)}) collective-permute-start(bf16[2,256,512]{2,1,0:T(8,128)(2,1)S(1)} %all_gather.7), channel_id=1, source_target_pairs={{0,4},{4,8},{8,12},{12,16},{16,20},{20,24},{24,28},{28,32},{32,36}... | collective-permute-start | bytes 1572872 | tf_op jit(solution)/shard_map/ppermute | solution.py:12
  104.7 5.8 %copy-start.1 = (bf16[3,256,128]{2,1,0:T(8,128)(2,1)S(1)}, bf16[3,256,128]{2,1,0:T(8,128)(2,1)}, u32[]{:S(2)}) copy-start(bf16[3,256,128]{2,1,0:T(8,128)(2,1)} %param.16) | copy-start | bytes 589828
Sparse Core Ops, SparseCore 0:
  51.3 31.8 reduce-scatter.1

commit v2 on v0

v2 whole, which is shorter than its diff:
```python
import jax
import jax.numpy as jnp
from jax import lax
from jax.experimental import pallas as pl
from jax.experimental.pallas import tpu as pltpu
from jax.sharding import PartitionSpec as P

MESH = pl.DeviceIdType.MESH
F32 = jnp.float32
BF16 = jnp.bfloat16
NQ = 8
NZ = 16
NX = 4
NT = NQ * NZ


def nt(a, b):
    return lax.dot_general(a, b, (((1,), (1,)), ((), ())), preferred_element_type=F32)


def nn(a, b):
    return lax.dot_general(a, b, (((1,), (0,)), ((), ())), preferred_element_type=F32)


def tn(a, b):
    return lax.dot_general(a, b, (((0,), (0,)), ((), ())), preferred_element_type=F32)


def kernel(
    clip_ref, video_ref, w1_ref, w2_ref, cot_ref,
    enc_ref, o1_ref, o2_ref,
    vext, coth, flags, flagh, uown, usend, urecv, pre, dsext,
    masks, part, send1, recv1, mine, recv2, gather, held,
    sva, rva, svb, rvb, svh, rvh, sct, rct, sfl, rfl, su, ru, sds, rds, sdh, rdh,
    sa, ra, sb, rb, sc, rc, sd, rd,
):
    me = lax.axis_index("tm")
    chan = lax.axis_index("chan")
    z, q = me // NQ, lax.rem(me, NQ)
    prev = (lax.rem(me + NT - 1, NT), chan)
    nxt = (lax.rem(me + 1, NT), chan)

    def in_z(s):
        return (z * NQ + lax.rem(q + s, NQ), chan)

    def over_z(s):
        return (lax.rem(z + s, NZ) * NQ + q, chan)

    def over_x(s):
        return (me, lax.rem(chan + s, NX))

    def signal(device):
        pl.semaphore_signal(barrier, inc=1, device_id=device, device_id_type=MESH)

    started = []

    def send(src, dst, ssem, rsem, device):
        copy = pltpu.make_async_remote_copy(
            src_ref=src, dst_ref=dst, send_sem=ssem, recv_sem=rsem,
            device_id=device, device_id_type=MESH,
        )
        copy.start()
        started.append(copy)
        return copy

    barrier = pltpu.get_barrier_semaphore()
    for s in range(1, NX):
        signal(over_x(s))
    signal(prev)
    signal(nxt)
    for s in range(1, NQ):
        signal(in_z(s))
    for s in range(1, NZ):
        signal(over_z(s))

    start = [clip_ref[t] - 4 * me for t in range(4)]
    start2 = [lax.shift_right_arithmetic(clip_ref[2 * j], 1) - 2 * me for j in range(2)]

    def flag(condition):
        return jnp.where(condition, 1.0, 0.0).astype(F32)

    rows = [start2[0] <= -1, start2[0] == -1, start2[0] <= -2, start2[1] <= -1]
    flags[...] = jnp.concatenate(
        [jnp.full((1, 512), flag(r), F32) for r in rows] + [jnp.zeros((12, 512), F32)], axis=0
    ).astype(BF16)

    def block(c, size):
        return pl.ds(pl.multiple_of(c * size, size), size)

    pl.semaphore_wait(barrier, (NX - 1) + 2 + (NQ - 1) + (NZ - 1))

    own = block(chan, 32)
    ahead = [None]
    for s in range(1, NX):
        ahead.append(send(video_ref.at[2:4], vext.at[4:6, own], sva.at[s], rva.at[s], over_x(s)))
    cot_copy = send(cot_ref, coth, sct, rct, prev)
    flag_copy = send(flags, flagh, sfl, rfl, prev)
    halo = [send(video_ref.at[2:4], vext.at[0:2, own], svh.at[0], rvh.at[0], nxt)]
    behind = [None]
    for s in range(1, NX):
        behind.append(send(video_ref.at[0:2], vext.at[2:4, own], svb.at[s], rvb.at[s], over_x(s)))
    vext[2:6, own, :] = video_ref[...]
    for s in range(1, NX):
        ahead[s].wait_recv()
        from_s = block(lax.rem(chan + NX - s, NX), 32)
        halo.append(send(vext.at[4:6, from_s], vext.at[0:2, from_s], svh.at[s], rvh.at[s], nxt))

    cot = [cot_ref[0], cot_ref[1]]

    def masked(x, condition):
        return x * flag(condition).astype(BF16)

    masks[0] = masked(cot[0], start2[0] == 0)
    masks[1] = masked(cot[1], start2[1] == 1)
    masks[2] = masked(cot[1], start2[1] <= 0)
    masks[3] = masked(cot[1], start2[1] == 0)
    a, b, c, d = (masks[i] for i in range(4))
    w2 = [w2_ref[k] for k in range(3)]
    local0 = nn(
        jnp.concatenate([w2[0], w2[1], w2[1], w2[2], w2[2]], axis=1),
        jnp.concatenate([cot[0], a, c, a, d], axis=0),
    )
    local1 = nn(
        jnp.concatenate([w2[0], w2[1], w2[2]], axis=1), jnp.concatenate([cot[1], b, b], axis=0)
    )
    cot_copy.wait_recv()
    flag_copy.wait_recv()
    later = [coth[0], coth[1]]
    for i in range(4):
        masks[4 + i] = later[i // 3] * flagh[i : i + 1, :]
    e, f, g, h = (masks[4 + i] for i in range(4))
    units = [
        local0 + nn(w2[2], g),
        local1 + nn(jnp.concatenate([w2[1], w2[2], w2[2]], axis=1), jnp.concatenate([e, f, h], axis=0)),
    ]
    for i in range(2):
        for x in range(NX):
            piece = units[i][64 * x : 64 * x + 64]
            uown[x, i] = piece
            usend[x, i] = piece.astype(BF16)
    sums = [None]
    for s in range(1, NX):
        sums.append(send(usend.at[lax.rem(chan + s, NX)], urecv.at[s], su.at[s], ru.at[s], over_x(s)))

    for s in range(1, NX):
        behind[s].wait_recv()
    for s in range(NX):
        halo[s].wait_recv()
    w1 = jnp.concatenate([w1_ref[k] for k in range(3)], axis=0)
    source = [[jnp.maximum(t - k, start[t]) + 2 for k in range(3)] for t in range(4)]
    mine64 = block(chan, 64)
    for j in range(2):
        total = None
        for t in (2 * j, 2 * j + 1):
            p = tn(w1, jnp.concatenate([vext[source[t][k]] for k in range(3)], axis=0))
            pre[t] = p
            act = p * jax.nn.sigmoid(p)
            total = act if total is None else total + act
        dsext[2 + j, mine64, :] = (0.5 * total).astype(BF16)
    spread = [None]
    for s in range(1, NX):
        spread.append(
            send(dsext.at[2:4, mine64], dsext.at[2:4, mine64], sds.at[s], rds.at[s], over_x(s))
        )
    dhalo = [send(dsext.at[2:4, mine64], dsext.at[0:2, mine64], sdh.at[0], rdh.at[0], nxt)]

    unit = uown[chan]
    for s in range(1, NX):
        sums[s].wait_recv()
        unit = unit + urecv[s].astype(F32)
    deltas = []
    for t in range(4):
        p = pre[t]
        sig = jax.nn.sigmoid(p)
        deltas.append((0.5 * unit[t // 2] * sig * (1.0 + p * (1.0 - sig))).astype(BF16))
    delta = jnp.concatenate(deltas, axis=1)
    for k in range(3):
        grad = nt(delta, jnp.concatenate([vext[source[t][k]] for t in range(4)], axis=1))
        part[6 + k // 2, 64 * (k % 2) : 64 * (k % 2) + 64, :] = grad
    part[7, 64:128, :] = jnp.zeros((64, 128), F32)

    for s in range(1, NX):
        spread[s].wait_recv()
        from_s = block(lax.rem(chan + NX - s, NX), 64)
        dhalo.append(send(dsext.at[2:4, from_s], dsext.at[0:2, from_s], sdh.at[s], rdh.at[s], nxt))
    cot = [cot_ref.at[0], cot_ref.at[1]]
    a, b, c, d, e, f, g, h = (masks.at[i] for i in range(8))
    terms = [
        [(0, cot[0]), (1, cot[1])],
        [(0, a), (1, b), (0, c), (1, e)],
        [(0, a), (1, b), (0, d), (1, f), (0, g), (1, h)],
    ]
    @pl.loop(0, 2)
    def _(half):
        for k in range(3):
            right = jnp.concatenate([v[...] for _, v in terms[k]], axis=1)
            left = [dsext[2 + i, block(half, 128), :] for i, _ in terms[k]]
            part[2 * k + half] = nt(jnp.concatenate(left, axis=1), right)

    send1[...] = part[...].astype(BF16)

    first = [None]
    for s in range(1, NQ):
        first.append(send(send1.at[lax.rem(q + s, NQ)], recv1.at[s], sa.at[s], ra.at[s], in_z(s)))

    for s in range(NX):
        dhalo[s].wait_recv()
    w2t = jnp.concatenate(w2, axis=0)
    for j in range(2):
        sources = [dsext[jnp.maximum(j - k, start2[j]) + 2] for k in range(3)]
        enc_ref[j] = tn(w2t, jnp.concatenate(sources, axis=0)).astype(BF16)

    total = part[q]
    for s in range(1, NQ):
        first[s].wait_recv()
        total = total + recv1[s].astype(F32)
    mine[...] = total.reshape(NZ, 8, 128)
    second = [None]
    for s in range(1, NZ):
        second.append(send(mine.at[lax.rem(z + s, NZ)], recv2.at[s], sb.at[s], rb.at[s], over_z(s)))
    total = mine[z]
    for s in range(1, NZ):
        second[s].wait_recv()
        total = total + recv2[s]
    gather[z] = total
    third = [send(gather.at[z], gather.at[z], sc.at[s], rc.at[s], over_z(s)) for s in range(1, NZ)]
    for copy in third:
        copy.wait_recv()
    held[q] = gather[...].reshape(128, 128).astype(BF16)
    fourth = [send(held.at[q], held.at[q], sd.at[s], rd.at[s], in_z(s)) for s in range(1, NQ)]
    for copy in fourth:
        copy.wait_recv()
    for k in range(3):
        o2_ref[k] = held[2 * k : 2 * k + 2].reshape(256, 128).astype(F32) * (131072.0 ** -0.5)
        piece = held[6 + k // 2, (k % 2) * 64 : (k % 2) * 64 + 64, :]
        o1_ref[k] = piece.astype(F32).T * (262144.0 ** -0.5)
    for copy in started:
        copy.wait_send()


def per_device(video, clip_start, first_conv_weight, second_conv_weight, cotangent):
    vmem = pl.BlockSpec(memory_space=pltpu.VMEM)
    smem = pl.BlockSpec(memory_space=pltpu.SMEM)
    dma = pltpu.SemaphoreType.DMA
    return pl.pallas_call(
        kernel,
        out_shape=(
            jax.ShapeDtypeStruct((2, 128, 512), BF16),
            jax.ShapeDtypeStruct((3, 128, 64), F32),
            jax.ShapeDtypeStruct((3, 256, 128), F32),
        ),
        in_specs=[smem, vmem, vmem, vmem, vmem],
        out_specs=(vmem, vmem, vmem),
        scratch_shapes=[
            pltpu.VMEM((6, 128, 512), BF16),
            pltpu.VMEM((2, 128, 512), BF16),
            pltpu.VMEM((16, 512), BF16),
            pltpu.VMEM((16, 512), BF16),
            pltpu.VMEM((NX, 2, 64, 512), F32),
            pltpu.VMEM((NX, 2, 64, 512), BF16),
            pltpu.VMEM((NX, 2, 64, 512), BF16),
            pltpu.VMEM((4, 64, 512), F32),
            pltpu.VMEM((4, 256, 512), BF16),
            pltpu.VMEM((8, 128, 512), BF16),
            pltpu.VMEM((NQ, 128, 128), F32),
            pltpu.VMEM((NQ, 128, 128), BF16),
            pltpu.VMEM((NQ, 128, 128), BF16),
            pltpu.VMEM((NZ, 8, 128), F32),
            pltpu.VMEM((NZ, 8, 128), F32),
            pltpu.VMEM((NZ, 8, 128), F32),
            pltpu.VMEM((NQ, 128, 128), BF16),
        ]
        + [dma((NX,))] * 6
        + [dma(())] * 4
        + [dma((NX,))] * 6
        + [dma((NQ,)), dma((NQ,)), dma((NZ,)), dma((NZ,)), dma((NZ,)), dma((NZ,)), dma((NQ,)), dma((NQ,))],
        compiler_params=pltpu.CompilerParams(
            collective_id=0, has_side_effects=True, vmem_limit_bytes=40 * 1024 * 1024
        ),
    )(clip_start, video, first_conv_weight, second_conv_weight, cotangent)


def solution(mesh):
    in_specs = (
        P("tm", "chan", None),
        P("tm"),
        P(None, None, "chan"),
        P(None, None, "chan"),
        P("tm", "chan", None),
    )
    out_specs = (P("tm", "chan", None), P(None, None, "chan"), P(None, None, "chan"))
    return jax.shard_map(
        per_device, mesh=mesh, in_specs=in_specs, out_specs=out_specs, check_vma=False
    )
```

time: 455 us -> 76.2 us (0.17)
  waiting for transfers between devices: 363 us -> 0 us
  Pallas kernels: 0 us -> 70.3 us
  blocking collectives: 22.9 us -> 0 us
  starting transfers between devices: 17.9 us -> 0 us
  matrix products: 17.3 us -> 0 us
  between operations: 14.4 us -> 0.69 us
  local copies, waits for them, and re-layouts: 12.3 us -> 5.03 us
  other arithmetic: 6.72 us -> 0 us
    psum x1 -> x0, waiting for transfers between devices: 329 us -> none  [per_device(): lax.psum((first_weight_gradient, second_weight_gradient), 'tm')]
    pallas_call x0 -> x1, Pallas kernels: none -> 70.3 us  [per_device(): pl.pallas_call(kernel, out_shape=(jax.ShapeDtypeStruct((2, 128, 512), BF1...]
    reduce_scatter x1 -> x0, waiting for transfers between devices: 29 us -> none  [per_device(): lax.psum_scatter(local_terms, 'chan', scatter_dimension=1, tiled=True)]
    all_gather x2 -> x0, blocking collectives: 22.9 us -> none  [the longest x1 11.6 us: per_device(): full_input = lax.all_gather(video, 'chan', axis=1, tiled=True)]
    ppermute x3 -> x0, starting transfers between devices: 17.8 us -> none  [passed_along(): return lax.ppermute(block, axis, route)]
    dot_general x18 -> x0, matrix products: 17.3 us -> none  [the longest x3 9.28 us: per_device(): jnp.einsum('ij,jcs->ics', selector, tap_contribution, precision=lax.Preci...]
    ppermute x3 -> x0, waiting for transfers between devices: 4.77 us -> none  [passed_along(): return lax.ppermute(block, axis, route)]
  transfers between devices with their start and end apart: 5 -> 0, of which waited for: 4 -> 0; matrix products, arithmetic and copies ran while one was open for 2% -> 0% of each run, Pallas kernels for 0% -> 0%
where the time goes in v2:
time: 76.2 us; the launch traced here: 76 us
  Pallas kernels  70.3 us (92%)
  local copies, waits for them, and re-layouts  5.03 us (7%)
    pallas_call x1, Pallas kernels, per_device(): pl.pallas_call(kernel, out_shape=(jax.ShapeDtypeStruct((2, 128, 512), BF1...  70.3 us
    unnamed x11, local copies, waits for them, and re-layouts  4.28 us

profile of v2, /device:TPU:1, one launch (start us, length us, event | category | flops | bytes accessed | tf_op | source)
XLA Modules:
  0.0 76.0 jit_solution(122102609336400308)
XLA Ops:
  0.6 0.0 copy-start.3
  0.6 0.0 copy-start.2
  0.7 0.9 %copy.8.w1_ref = bf16[3,128,64]{2,1,0:T(8,128)(2,1)S(1)} copy(bf16[3,128,64]{1,2,0:T(8,128)(2,1)} %param.7) | data formatting | bytes 98304 | tf_op args[2]
  1.6 0.0 copy-done.3
  1.6 0.0 copy-done.2
  1.6 0.0 copy-start
  1.6 0.9 %copy-done = bf16[2,128,512]{2,1,0:T(8,128)(2,1)S(1)} copy-done((bf16[2,128,512]{2,1,0:T(8,128)(2,1)S(1)}, bf16[2,128,512]{2,1,0:T(8,128)(2,1)}, u32[]{:S(2)}) %copy-start) | copy-done | bytes 262168
  2.6 0.0 copy-start.1
  2.6 0.9 %copy-done.1 = bf16[3,256,128]{2,1,0:T(8,128)(2,1)S(1)} copy-done((bf16[3,256,128]{2,1,0:T(8,128)(2,1)S(1)}, bf16[3,256,128]{2,1,0:T(8,128)(2,1)}, u32[]{:S(2)}) %copy-start.1) | copy-done | bytes 196632
  3.5 70.3 %shard_map.76 = (bf16[2,128,512]{2,1,0:T(8,128)(2,1)S(1)}, f32[3,128,64]{2,1,0:T(8,128)S(1)}, f32[3,256,128]{2,1,0:T(8,128)S(1)}) custom-call(s32[4]{0:T(128)S(1)} %copy-done.3, bf16[4,32,512]{2,1,0:T(8,128)(2,1)S(1)} %copy-done.2, bf16[3,128,64]{2,1,0:T(8,128)(2,1)S(1)} %copy.8.w1_ref, bf16[3,256,128]{2,1,0:T(8,128)(2,1)S(1)} %copy-done.1, ...), custom_call_target="tpu_custom_call" | custom-call | tf_op jit(solution)/shard_map/pallas_call | solution.py:245
  73.8 0.8 copy.9
  74.6 0.7 copy.12
  75.3 0.7 copy.13
Async XLA Ops:
  0.6 1.0 %copy-start.3 = (s32[4]{0:T(128)S(1)}, s32[4]{0:T(128)}, u32[]{:S(2)}) copy-start(s32[4]{0:T(128)} %clip_ref.1) | copy-start | bytes 52
  0.6 1.0 %copy-start.2 = (bf16[4,32,512]{2,1,0:T(8,128)(2,1)S(1)}, bf16[4,32,512]{2,1,0:T(8,128)(2,1)}, u32[]{:S(2)}) copy-start(bf16[4,32,512]{2,1,0:T(8,128)(2,1)} %video_ref.1) | copy-start | bytes 393220
  1.6 1.0 %copy-start = (bf16[2,128,512]{2,1,0:T(8,128)(2,1)S(1)}, bf16[2,128,512]{2,1,0:T(8,128)(2,1)}, u32[]{:S(2)}) copy-start(bf16[2,128,512]{2,1,0:T(8,128)(2,1)} %cot_ref.1) | copy-start | bytes 786436
  2.6 0.9 %copy-start.1 = (bf16[3,256,128]{2,1,0:T(8,128)(2,1)S(1)}, bf16[3,256,128]{2,1,0:T(8,128)(2,1)}, u32[]{:S(2)}) copy-start(bf16[3,256,128]{2,1,0:T(8,128)(2,1)} %w2_ref.1) | copy-start | bytes 589828

commit v3 on v2

v3 whole, which is shorter than its diff:
```python
import jax
import jax.numpy as jnp
from jax import lax
from jax.experimental import pallas as pl
from jax.experimental.pallas import tpu as pltpu
from jax.sharding import PartitionSpec as P

MESH = pl.DeviceIdType.MESH
F32 = jnp.float32
BF16 = jnp.bfloat16
NQ = 8
NZ = 16
NX = 4
NT = NQ * NZ


def nt(a, b):
    return lax.dot_general(a, b, (((1,), (1,)), ((), ())), preferred_element_type=F32)


def nn(a, b):
    return lax.dot_general(a, b, (((1,), (0,)), ((), ())), preferred_element_type=F32)


def tn(a, b):
    return lax.dot_general(a, b, (((0,), (0,)), ((), ())), preferred_element_type=F32)


def kernel(
    clip_hbm, video_hbm, w1_hbm, w2_hbm, cot_hbm,
    enc_ref, held,
    clip_ref, w1_ref, w2_ref, cot_ref,
    vown, vhalo, coth, flags, flagh, uown, usend, urecv, pre, dsext,
    masks, part, send1, recv1, tiles, recv2, final,
    sin, sva, rva, svb, rvb, svh, rvh, sct, rct, sfl, rfl, su, ru, sds, rds, sdh, rdh,
    sa, ra, sb, rb, sc, rc, sd, rd, known,
):
    me = lax.axis_index("tm")
    chan = lax.axis_index("chan")
    z, q = me // NQ, lax.rem(me, NQ)
    prev = (lax.rem(me + NT - 1, NT), chan)
    nxt = (lax.rem(me + 1, NT), chan)

    def in_z(s):
        return (z * NQ + lax.rem(q + s, NQ), chan)

    def over_z(s):
        return (lax.rem(z + s, NZ) * NQ + q, chan)

    def over_x(s):
        return (me, lax.rem(chan + s, NX))

    def block(c, size):
        return pl.ds(pl.multiple_of(c * size, size), size)

    def remote(src, dst, ssem, rsem, device):
        return pltpu.make_async_remote_copy(
            src_ref=src, dst_ref=dst, send_sem=ssem, recv_sem=rsem,
            device_id=device, device_id_type=MESH,
        )

    started = []

    def send(src, dst, ssem, rsem, device):
        copy = remote(src, dst, ssem, rsem, device)
        copy.start()
        started.append(copy)
        return copy

    barrier = pltpu.get_barrier_semaphore()
    near = [over_x(s) for s in range(1, NX)] + [prev, nxt, over_z(1), over_z(NZ - 1)]
    near += [in_z(s) for s in range(1, NQ)]
    for device in near:
        pl.semaphore_signal(barrier, inc=1, device_id=device, device_id_type=MESH)

    own = block(chan, 32)
    fetch = [
        pltpu.make_async_copy(src, dst, sin.at[i])
        for i, (src, dst) in enumerate([
            (clip_hbm, clip_ref), (cot_hbm, cot_ref), (w2_hbm, w2_ref), (w1_hbm, w1_ref),
            (video_hbm, vown.at[:, own]),
        ])
    ]
    for copy in fetch:
        copy.start()
    fetch[0].wait()

    start = [clip_ref[t] - 4 * me for t in range(4)]
    start2 = [lax.shift_right_arithmetic(clip_ref[2 * j], 1) - 2 * me for j in range(2)]

    def flag(condition):
        return jnp.where(condition, 1.0, 0.0).astype(F32)

    rows = [start2[0] <= -1, start2[0] == -1, start2[0] <= -2, start2[1] <= -1]
    flags[...] = jnp.concatenate(
        [jnp.full((1, 512), flag(r), F32) for r in rows] + [jnp.zeros((12, 512), F32)], axis=0
    ).astype(BF16)

    pl.semaphore_wait(barrier, len(near))

    ahead, behind, halo = [None], [None], []
    for s in range(1, NX):
        ahead.append(send(video_hbm.at[2:4], vown.at[2:4, own], sva.at[s], rva.at[s], over_x(s)))
    halo.append(send(video_hbm.at[2:4], vhalo.at[:, own], svh.at[0], rvh.at[0], nxt))
    for s in range(1, NX):
        behind.append(send(video_hbm.at[0:2], vown.at[0:2, own], svb.at[s], rvb.at[s], over_x(s)))
    cot_copy = send(cot_hbm, coth, sct, rct, prev)
    flag_copy = send(flags, flagh, sfl, rfl, prev)

    def greet(step, distance):
        for s in (distance, NZ - distance):
            pl.semaphore_signal(known.at[step], inc=1, device_id=over_z(s), device_id_type=MESH)

    greet(0, 1)

    for copy in fetch[1:]:
        copy.wait()

    def masked(x, condition):
        return x * flag(condition).astype(BF16)

    cot = [cot_ref[0], cot_ref[1]]
    masks[0] = masked(cot[0], start2[0] == 0)
    masks[1] = masked(cot[1], start2[1] == 1)
    masks[2] = masked(cot[1], start2[1] <= 0)
    masks[3] = masked(cot[1], start2[1] == 0)
    a, b, c, d = (masks[i] for i in range(4))
    w2 = [w2_ref[k] for k in range(3)]
    local0 = nn(
        jnp.concatenate([w2[0], w2[1], w2[1], w2[2], w2[2]], axis=1),
        jnp.concatenate([cot[0], a, c, a, d], axis=0),
    )
    local1 = nn(
        jnp.concatenate([w2[0], w2[1], w2[2]], axis=1), jnp.concatenate([cot[1], b, b], axis=0)
    )
    cot_copy.wait_recv()
    flag_copy.wait_recv()
    for i in range(4):
        masks[4 + i] = coth[i // 3] * flagh[i : i + 1, :]
    e, f, g, h = (masks[4 + i] for i in range(4))
    units = [
        local0 + nn(w2[2], g),
        local1 + nn(jnp.concatenate([w2[1], w2[2], w2[2]], axis=1), jnp.concatenate([e, f, h], axis=0)),
    ]
    for i in range(2):
        for x in range(NX):
            piece = units[i][64 * x : 64 * x + 64]
            uown[x, i] = piece
            usend[x, i] = piece.astype(BF16)

    pl.semaphore_wait(known.at[0], 2)
    greet(1, 2)

    for s in range(1, NX):
        ahead[s].wait_recv()
        from_s = block(lax.rem(chan + NX - s, NX), 32)
        halo.append(send(vown.at[2:4, from_s], vhalo.at[:, from_s], svh.at[s], rvh.at[s], nxt))
    for s in range(1, NX):
        behind[s].wait_recv()
    sums = [None]
    for s in range(1, NX):
        sums.append(send(usend.at[lax.rem(chan + s, NX)], urecv.at[s], su.at[s], ru.at[s], over_x(s)))
    pl.semaphore_wait(known.at[1], 2)
    greet(2, 4)

    w1 = jnp.concatenate([w1_ref[k] for k in range(3)], axis=1)
    mine64 = block(chan, 64)

    def source(t, k):
        if k == 0:
            return vown[t]
        index = jnp.maximum(t - k, start[t])
        inside = vown[jnp.maximum(index, 0)]
        if t >= k:
            return inside
        return jnp.where(index < 0, vhalo[jnp.clip(index + 2, 0, 1)], inside)

    spread, dhalo = {}, {}
    for j in (1, 0):
        if j == 0:
            for s in range(NX):
                halo[s].wait_recv()
        total = None
        for t in (2 * j, 2 * j + 1):
            p = nn(w1, jnp.concatenate([source(t, k) for k in range(3)], axis=0))
            pre[t] = p
            act = p * jax.nn.sigmoid(p)
            total = act if total is None else total + act
        dsext[2 + j, mine64, :] = (0.5 * total).astype(BF16)
        row = dsext.at[2 + j, mine64]
        for s in range(1, NX):
            spread[j, s] = send(row, row, sds.at[j, s], rds.at[j, s], over_x(s))
    dhalo[0] = send(dsext.at[2:4, mine64], dsext.at[0:2, mine64], sdh.at[0], rdh.at[0], nxt)

    def hand_over(piece):
        send1[piece] = part[piece].astype(BF16)
        s = lax.rem(piece + NQ - q, NQ)

        @pl.when(s != 0)
        def _():
            remote(send1.at[piece], recv1.at[s], sa.at[piece], ra.at[s], (z * NQ + piece, chan)).start()

    unit = uown[chan]
    for s in range(1, NX):
        sums[s].wait_recv()
        unit = unit + urecv[s].astype(F32)
    deltas = []
    for t in range(4):
        p = pre[t]
        sig = jax.nn.sigmoid(p)
        deltas.append((0.5 * unit[t // 2] * sig * (1.0 + p * (1.0 - sig))).astype(BF16))
    delta = jnp.concatenate(deltas, axis=1)
    for k in range(3):
        grad = nt(delta, jnp.concatenate([source(t, k) for t in range(4)], axis=1))
        part[6 + k // 2, 64 * (k % 2) : 64 * (k % 2) + 64, :] = grad
    part[7, 64:128, :] = jnp.zeros((64, 128), F32)
    hand_over(6)
    hand_over(7)
    pl.semaphore_wait(known.at[2], 2)

    for s in range(1, NX):
        from_s = block(lax.rem(chan + NX - s, NX), 64)
        for j in (1, 0):
            spread[j, s].wait_recv()
        dhalo[s] = send(dsext.at[2:4, from_s], dsext.at[0:2, from_s], sdh.at[s], rdh.at[s], nxt)
    cot = [cot_ref.at[0], cot_ref.at[1]]
    a, b, c, d, e, f, g, h = (masks.at[i] for i in range(8))
    terms = [
        [(0, cot[0]), (1, cot[1])],
        [(0, a), (1, b), (0, c), (1, e)],
        [(0, a), (1, b), (0, d), (1, f), (0, g), (1, h)],
    ]

    @pl.loop(0, 2)
    def _(half):
        for k in range(3):
            right = jnp.concatenate([v[...] for _, v in terms[k]], axis=1)
            left = [dsext[2 + i, block(half, 128), :] for i, _ in terms[k]]
            part[2 * k + half] = nt(jnp.concatenate(left, axis=1), right)
            hand_over(2 * k + half)

    for s in range(NX):
        dhalo[s].wait_recv()
    w2t = jnp.concatenate([w2_ref[k] for k in range(3)], axis=0)
    for j in range(2):
        sources = [dsext[jnp.maximum(j - k, start2[j]) + 2] for k in range(3)]
        enc_ref[j] = tn(w2t, jnp.concatenate(sources, axis=0)).astype(BF16)

    total = part[q]
    for s in range(1, NQ):
        remote(send1.at[0], recv1.at[s], sa.at[0], ra.at[s], in_z(s)).wait_recv()
        total = total + recv1[s].astype(F32)
    tiles[...] = total.astype(BF16).reshape(8, 16, 128)

    owner = lax.rem(z + q, 2) == 0
    mine = z // 2

    def tile_of(s):
        return lax.rem(z + s, NZ) // 2

    @pl.when(owner)
    def _():
        first = [
            remote(tiles.at[tile_of(s)], recv2.at[s], sb.at[s], rb.at[s], over_z(s))
            for s in range(1, NZ)
        ]
        for s in range(2, NZ, 2):
            first[s - 1].start()
        total = tiles[mine].astype(F32)
        for s in range(1, NZ):
            first[s - 1].wait_recv()
            total = total + recv2[s].astype(F32)
        final[mine] = total.astype(BF16)
        second = [
            remote(final.at[mine], final.at[mine], sc.at[s], rc.at[s], over_z(s))
            for s in range(1, NZ)
        ]
        for copy in second:
            copy.start()
        for s in range(2, NZ, 2):
            second[s - 1].wait_recv()
            first[s - 1].wait_send()
        for copy in second:
            copy.wait_send()

    @pl.when(jnp.logical_not(owner))
    def _():
        first = [
            remote(tiles.at[tile_of(s)], recv2.at[s], sb.at[s], rb.at[s], over_z(s))
            for s in range(1, NZ, 2)
        ]
        for copy in first:
            copy.start()
        for s in range(1, NZ, 2):
            remote(final.at[mine], final.at[mine], sc.at[s], rc.at[s], over_z(s)).wait_recv()
        for copy in first:
            copy.wait_send()

    held[q] = final[...].reshape(128, 128)
    fourth = [send(held.at[q], held.at[q], sd.at[s], rd.at[s], in_z(s)) for s in range(1, NQ)]
    for piece in range(NQ):
        @pl.when(piece != q)
        def _():
            remote(send1.at[piece], recv1.at[1], sa.at[piece], ra.at[1], nxt).wait_send()
    for copy in fourth:
        copy.wait_recv()
    for copy in started:
        copy.wait_send()


def write_kernel(enc_ref, held, out_ref, o1_ref, o2_ref):
    out_ref[...] = enc_ref[...]
    for k in range(3):
        o2_ref[k] = held[2 * k : 2 * k + 2].reshape(256, 128).astype(F32) * (131072.0 ** -0.5)
        piece = held[6 + k // 2, (k % 2) * 64 : (k % 2) * 64 + 64, :]
        o1_ref[k] = piece.astype(F32) * (262144.0 ** -0.5)


def per_device(video, clip_start, first_conv_weight, second_conv_weight, cotangent):
    vmem = pl.BlockSpec(memory_space=pltpu.VMEM)
    hbm = pl.BlockSpec(memory_space=pltpu.HBM)
    dma = pltpu.SemaphoreType.DMA
    encoded, held = pl.pallas_call(
        kernel,
        out_shape=(
            jax.ShapeDtypeStruct((2, 128, 512), BF16),
            jax.ShapeDtypeStruct((NQ, 128, 128), BF16),
        ),
        in_specs=[hbm] * 5,
        out_specs=(vmem, vmem),
        scratch_shapes=[
            pltpu.SMEM((4,), jnp.int32),
            pltpu.VMEM((3, 64, 128), BF16),
            pltpu.VMEM((3, 256, 128), BF16),
            pltpu.VMEM((2, 128, 512), BF16),
            pltpu.VMEM((4, 128, 512), BF16),
            pltpu.VMEM((2, 128, 512), BF16),
            pltpu.VMEM((2, 128, 512), BF16),
            pltpu.VMEM((16, 512), BF16),
            pltpu.VMEM((16, 512), BF16),
            pltpu.VMEM((NX, 2, 64, 512), F32),
            pltpu.VMEM((NX, 2, 64, 512), BF16),
            pltpu.VMEM((NX, 2, 64, 512), BF16),
            pltpu.VMEM((4, 64, 512), F32),
            pltpu.VMEM((4, 256, 512), BF16),
            pltpu.VMEM((8, 128, 512), BF16),
            pltpu.VMEM((NQ, 128, 128), F32),
            pltpu.VMEM((NQ, 128, 128), BF16),
            pltpu.VMEM((NQ, 128, 128), BF16),
            pltpu.VMEM((8, 16, 128), BF16),
            pltpu.VMEM((NZ, 16, 128), BF16),
            pltpu.VMEM((8, 16, 128), BF16),
            dma((5,)),
        ]
        + [dma((NX,))] * 6
        + [dma(())] * 4
        + [dma((NX,))] * 2
        + [dma((2, NX))] * 2
        + [dma((NX,))] * 2
        + [dma((NQ,)), dma((NQ,)), dma((NZ,)), dma((NZ,)), dma((NZ,)), dma((NZ,)), dma((NQ,)), dma((NQ,))]
        + [pltpu.SemaphoreType.REGULAR((3,))],
        compiler_params=pltpu.CompilerParams(
            collective_id=0, has_side_effects=True, vmem_limit_bytes=62 * 1024 * 1024
        ),
    )(clip_start, video, first_conv_weight.transpose(0, 2, 1), second_conv_weight, cotangent)
    encoded, first_grad, second_grad = pl.pallas_call(
        write_kernel,
        out_shape=(
            jax.ShapeDtypeStruct((2, 128, 512), BF16),
            jax.ShapeDtypeStruct((3, 64, 128), F32),
            jax.ShapeDtypeStruct((3, 256, 128), F32),
        ),
        in_specs=[vmem] * 2,
        out_specs=(vmem,) * 3,
    )(encoded, held)
    return encoded, first_grad.transpose(0, 2, 1), second_grad


def solution(mesh):
    in_specs = (
        P("tm", "chan", None),
        P("tm"),
        P(None, None, "chan"),
        P(None, None, "chan"),
        P("tm", "chan", None),
    )
    out_specs = (P("tm", "chan", None), P(None, None, "chan"), P(None, None, "chan"))
    return jax.shard_map(
        per_device, mesh=mesh, in_specs=in_specs, out_specs=out_specs, check_vma=False
    )
```

time: 76.2 us -> 66 us (0.87)
  Pallas kernels: 70.3 us -> 64.6 us
  local copies, waits for them, and re-layouts: 5.03 us -> 0 us
    pallas_call x1, Pallas kernels: 70.3 us -> 62.6 us  [per_device(): pl.pallas_call(kernel, out_shape=(jax.ShapeDtypeStruct((2, 128, 512), BF1...]
    unnamed x11 -> x0, local copies, waits for them, and re-layouts: 4.28 us -> none
    pallas_call x0 -> x1, Pallas kernels: none -> 1.91 us  [per_device(): pl.pallas_call(write_kernel, out_shape=(jax.ShapeDtypeStruct((2, 128, 512...]
where the time goes in v3:
time: 66 us; the launch traced here: 65.2 us
  Pallas kernels  64.6 us (98%)
    pallas_call x1, Pallas kernels, per_device(): pl.pallas_call(kernel, out_shape=(jax.ShapeDtypeStruct((2, 128, 512), BF1...  62.6 us
    pallas_call x1, Pallas kernels, per_device(): pl.pallas_call(write_kernel, out_shape=(jax.ShapeDtypeStruct((2, 128, 512...  1.91 us

profile of v3, /device:TPU:1, one launch (start us, length us, event | category | flops | bytes accessed | tf_op | source)
XLA Modules:
  0.0 65.2 jit_solution(9941595966831949584)
XLA Ops:
  0.6 62.6 %shard_map.76 = (bf16[2,128,512]{2,1,0:T(8,128)(2,1)}, bf16[8,128,128]{2,1,0:T(8,128)(2,1)}) custom-call(s32[4]{0:T(128)} %clip_hbm.1, bf16[4,32,512]{2,1,0:T(8,128)(2,1)} %video_hbm.1, bf16[3,64,128]{2,1,0:T(8,128)(2,1)} %bitcast.2, bf16[3,256,128]{2,1,0:T(8,128)(2,1)} %w2_hbm.1, bf16[2,128,512]{2,1,0:T(8,128)(2,1)} %cot_hbm.1), custom_call_target="tpu_custom_call" | custom-call | tf_op jit(solution)/shard_map/pallas_call | solution.py:323
  63.3 1.9 %shard_map.77 = (bf16[2,128,512]{2,1,0:T(8,128)(2,1)}, f32[3,64,128]{2,1,0:T(8,128)}, f32[3,256,128]{2,1,0:T(8,128)}) custom-call(bf16[2,128,512]{2,1,0:T(8,128)(2,1)} %get-tuple-element.8.enc_ref, bf16[8,128,128]{2,1,0:T(8,128)(2,1)} %get-tuple-element.9.held), custom_call_target="tpu_custom_call" | custom-call | tf_op jit(solution)/shard_map/pallas_call | solution.py:366

commit v4 on v3

--- a/solution.py
+++ b/solution.py
@@ -32,7 +32,7 @@
     clip_ref, w1_ref, w2_ref, cot_ref,
     vown, vhalo, coth, flags, flagh, uown, usend, urecv, pre, dsext,
     masks, part, send1, recv1, tiles, recv2, final,
-    sin, sva, rva, svb, rvb, svh, rvh, sct, rct, sfl, rfl, su, ru, sds, rds, sdh, rdh,
+    sin, sva, rva, svb, rvb, svh, rvh, sct, rct, sfl, rfl, su, ru, sw, rw, sdh, rdh,
     sa, ra, sb, rb, sc, rc, sd, rd, known,
 ):
     me = lax.axis_index("tm")
@@ -73,11 +73,11 @@
     for device in near:
         pl.semaphore_signal(barrier, inc=1, device_id=device, device_id_type=MESH)
 
-    own = block(chan, 32)
+    own, mine64 = block(chan, 32), block(chan, 64)
     fetch = [
         pltpu.make_async_copy(src, dst, sin.at[i])
         for i, (src, dst) in enumerate([
-            (clip_hbm, clip_ref), (cot_hbm, cot_ref), (w2_hbm, w2_ref), (w1_hbm, w1_ref),
+            (clip_hbm, clip_ref), (cot_hbm, cot_ref), (w2_hbm, w2_ref), (w1_hbm, w1_ref.at[:, mine64]),
             (video_hbm, vown.at[:, own]),
         ])
     ]
@@ -102,6 +102,9 @@
     for s in range(1, NX):
         ahead.append(send(video_hbm.at[2:4], vown.at[2:4, own], sva.at[s], rva.at[s], over_x(s)))
     halo.append(send(video_hbm.at[2:4], vhalo.at[:, own], svh.at[0], rvh.at[0], nxt))
+    weights = [None]
+    for s in range(1, NX):
+        weights.append(send(w1_hbm, w1_ref.at[:, mine64], sw.at[s], rw.at[s], over_x(s)))
     for s in range(1, NX):
         behind.append(send(video_hbm.at[0:2], vown.at[0:2, own], svb.at[s], rvb.at[s], over_x(s)))
     cot_copy = send(cot_hbm, coth, sct, rct, prev)
@@ -163,8 +166,9 @@
     pl.semaphore_wait(known.at[1], 2)
     greet(2, 4)
 
+    for s in range(1, NX):
+        weights[s].wait_recv()
     w1 = jnp.concatenate([w1_ref[k] for k in range(3)], axis=1)
-    mine64 = block(chan, 64)
 
     def source(t, k):
         if k == 0:
@@ -175,7 +179,6 @@
             return inside
         return jnp.where(index < 0, vhalo[jnp.clip(index + 2, 0, 1)], inside)
 
-    spread, dhalo = {}, {}
     for j in (1, 0):
         if j == 0:
             for s in range(NX):
@@ -186,11 +189,7 @@
             pre[t] = p
             act = p * jax.nn.sigmoid(p)
             total = act if total is None else total + act
-        dsext[2 + j, mine64, :] = (0.5 * total).astype(BF16)
-        row = dsext.at[2 + j, mine64]
-        for s in range(1, NX):
-            spread[j, s] = send(row, row, sds.at[j, s], rds.at[j, s], over_x(s))
-    dhalo[0] = send(dsext.at[2:4, mine64], dsext.at[0:2, mine64], sdh.at[0], rdh.at[0], nxt)
+        dsext[2 + j] = (0.5 * total).astype(BF16)
 
     def hand_over(piece):
         send1[piece] = part[piece].astype(BF16)
@@ -199,6 +198,22 @@
         @pl.when(s != 0)
         def _():
             remote(send1.at[piece], recv1.at[s], sa.at[piece], ra.at[s], (z * NQ + piece, chan)).start()
+
+    cot = [cot_ref.at[0], cot_ref.at[1]]
+    a, b, c, d, e, f, g, h = (masks.at[i] for i in range(8))
+    terms = [
+        [(0, cot[0]), (1, cot[1])],
+        [(0, a), (1, b), (0, c), (1, e)],
+        [(0, a), (1, b), (0, d), (1, f), (0, g), (1, h)],
+    ]
+
+    @pl.loop(0, 2)
+    def _(half):
+        for k in range(3):
+            right = jnp.concatenate([v[...] for _, v in terms[k]], axis=1)
+            left = [dsext[2 + i, block(half, 128), :] for i, _ in terms[k]]
+            part[2 * k + half] = nt(jnp.concatenate(left, axis=1), right)
+            hand_over(2 * k + half)
 
     unit = uown[chan]
     for s in range(1, NX):
@@ -206,7 +221,7 @@
         unit = unit + urecv[s].astype(F32)
     deltas = []
     for t in range(4):
-        p = pre[t]
+        p = pre[t, mine64, :]
         sig = jax.nn.sigmoid(p)
         deltas.append((0.5 * unit[t // 2] * sig * (1.0 + p * (1.0 - sig))).astype(BF16))
     delta = jnp.concatenate(deltas, axis=1)
@@ -216,35 +231,8 @@
     part[7, 64:128, :] = jnp.zeros((64, 128), F32)
     hand_over(6)
     hand_over(7)
+    dhalo = send(dsext.at[2:4], dsext.at[0:2], sdh, rdh, nxt)
     pl.semaphore_wait(known.at[2], 2)
-
-    for s in range(1, NX):
-        from_s = block(lax.rem(chan + NX - s, NX), 64)
-        for j in (1, 0):
-            spread[j, s].wait_recv()
-        dhalo[s] = send(dsext.at[2:4, from_s], dsext.at[0:2, from_s], sdh.at[s], rdh.at[s], nxt)
-    cot = [cot_ref.at[0], cot_ref.at[1]]
-    a, b, c, d, e, f, g, h = (masks.at[i] for i in range(8))
-    terms = [
-        [(0, cot[0]), (1, cot[1])],
-        [(0, a), (1, b), (0, c), (1, e)],
-        [(0, a), (1, b), (0, d), (1, f), (0, g), (1, h)],
-    ]
-
-    @pl.loop(0, 2)
-    def _(half):
-        for k in range(3):
-            right = jnp.concatenate([v[...] for _, v in terms[k]], axis=1)
-            left = [dsext[2 + i, block(half, 128), :] for i, _ in terms[k]]
-            part[2 * k + half] = nt(jnp.concatenate(left, axis=1), right)
-            hand_over(2 * k + half)
-
-    for s in range(NX):
-        dhalo[s].wait_recv()
-    w2t = jnp.concatenate([w2_ref[k] for k in range(3)], axis=0)
-    for j in range(2):
-        sources = [dsext[jnp.maximum(j - k, start2[j]) + 2] for k in range(3)]
-        enc_ref[j] = tn(w2t, jnp.concatenate(sources, axis=0)).astype(BF16)
 
     total = part[q]
     for s in range(1, NQ):
@@ -258,43 +246,48 @@
     def tile_of(s):
         return lax.rem(z + s, NZ) // 2
 
+    def to_owner(s):
+        return remote(tiles.at[tile_of(s)], recv2.at[s], sb.at[s], rb.at[s], over_z(s))
+
+    def from_owner(s):
+        return remote(final.at[mine], final.at[mine], sc.at[s], rc.at[s], over_z(s))
+
     @pl.when(owner)
     def _():
-        first = [
-            remote(tiles.at[tile_of(s)], recv2.at[s], sb.at[s], rb.at[s], over_z(s))
-            for s in range(1, NZ)
-        ]
         for s in range(2, NZ, 2):
-            first[s - 1].start()
+            to_owner(s).start()
+
+    @pl.when(jnp.logical_not(owner))
+    def _():
+        for s in range(1, NZ, 2):
+            to_owner(s).start()
+
+    dhalo.wait_recv()
+    w2t = jnp.concatenate([w2_ref[k] for k in range(3)], axis=0)
+    for j in range(2):
+        sources = [dsext[jnp.maximum(j - k, start2[j]) + 2] for k in range(3)]
+        enc_ref[j] = tn(w2t, jnp.concatenate(sources, axis=0)).astype(BF16)
+
+    @pl.when(owner)
+    def _():
         total = tiles[mine].astype(F32)
         for s in range(1, NZ):
-            first[s - 1].wait_recv()
+            to_owner(s).wait_recv()
             total = total + recv2[s].astype(F32)
         final[mine] = total.astype(BF16)
-        second = [
-            remote(final.at[mine], final.at[mine], sc.at[s], rc.at[s], over_z(s))
-            for s in range(1, NZ)
-        ]
-        for copy in second:
-            copy.start()
+        for s in range(1, NZ):
+            from_owner(s).start()
         for s in range(2, NZ, 2):
-            second[s - 1].wait_recv()
-            first[s - 1].wait_send()
-        for copy in second:
-            copy.wait_send()
+            from_owner(s).wait_recv()
+            to_owner(s).wait_send()
+        for s in range(1, NZ):
+            from_owner(s).wait_send()
 
     @pl.when(jnp.logical_not(owner))
     def _():
-        first = [
-            remote(tiles.at[tile_of(s)], recv2.at[s], sb.at[s], rb.at[s], over_z(s))
-            for s in range(1, NZ, 2)
-        ]
-        for copy in first:
-            copy.start()
         for s in range(1, NZ, 2):
-            remote(final.at[mine], final.at[mine], sc.at[s], rc.at[s], over_z(s)).wait_recv()
-        for copy in first:
-            copy.wait_send()
+            from_owner(s).wait_recv()
+            to_owner(s).wait_send()
 
     held[q] = final[...].reshape(128, 128)
     fourth = [send(held.at[q], held.at[q], sd.at[s], rd.at[s], in_z(s)) for s in range(1, NQ)]
@@ -330,7 +323,7 @@
         out_specs=(vmem, vmem),
         scratch_shapes=[
             pltpu.SMEM((4,), jnp.int32),
-            pltpu.VMEM((3, 64, 128), BF16),
+            pltpu.VMEM((3, 256, 128), BF16),
             pltpu.VMEM((3, 256, 128), BF16),
             pltpu.VMEM((2, 128, 512), BF16),
             pltpu.VMEM((4, 128, 512), BF16),
@@ -341,7 +334,7 @@
             pltpu.VMEM((NX, 2, 64, 512), F32),
             pltpu.VMEM((NX, 2, 64, 512), BF16),
             pltpu.VMEM((NX, 2, 64, 512), BF16),
-            pltpu.VMEM((4, 64, 512), F32),
+            pltpu.VMEM((4, 256, 512), F32),
             pltpu.VMEM((4, 256, 512), BF16),
             pltpu.VMEM((8, 128, 512), BF16),
             pltpu.VMEM((NQ, 128, 128), F32),
@@ -354,9 +347,8 @@
         ]
         + [dma((NX,))] * 6
         + [dma(())] * 4
-        + [dma((NX,))] * 2
-        + [dma((2, NX))] * 2
-        + [dma((NX,))] * 2
+        + [dma((NX,))] * 4
+        + [dma(())] * 2
         + [dma((NQ,)), dma((NQ,)), dma((NZ,)), dma((NZ,)), dma((NZ,)), dma((NZ,)), dma((NQ,)), dma((NQ,))]
         + [pltpu.SemaphoreType.REGULAR((3,))],
         compiler_params=pltpu.CompilerParams(

time: 66 us -> 59 us (0.89)
  Pallas kernels: 64.6 us -> 58.2 us
    pallas_call x1, Pallas kernels: 62.6 us -> 56.3 us  [per_device(): pl.pallas_call(kernel, out_shape=(jax.ShapeDtypeStruct((2, 128, 512), BF1...]
where the time goes in v4:
time: 59 us; the launch traced here: 58.9 us
  Pallas kernels  58.2 us (99%)
  between operations  0.64 us (1%)
    pallas_call x1, Pallas kernels, per_device(): pl.pallas_call(kernel, out_shape=(jax.ShapeDtypeStruct((2, 128, 512), BF1...  56.3 us
    pallas_call x1, Pallas kernels, per_device(): pl.pallas_call(write_kernel, out_shape=(jax.ShapeDtypeStruct((2, 128, 512...  1.91 us

profile of v4, /device:TPU:1, one launch (start us, length us, event | category | flops | bytes accessed | tf_op | source)
XLA Modules:
  0.0 58.9 jit_solution(17684380196473981732)
XLA Ops:
  0.6 56.3 %shard_map.76 = (bf16[2,128,512]{2,1,0:T(8,128)(2,1)}, bf16[8,128,128]{2,1,0:T(8,128)(2,1)}) custom-call(s32[4]{0:T(128)} %clip_hbm.1, bf16[4,32,512]{2,1,0:T(8,128)(2,1)} %video_hbm.1, bf16[3,64,128]{2,1,0:T(8,128)(2,1)} %bitcast.2, bf16[3,256,128]{2,1,0:T(8,128)(2,1)} %w2_hbm.1, bf16[2,128,512]{2,1,0:T(8,128)(2,1)} %cot_hbm.1), custom_call_target="tpu_custom_call" | custom-call | tf_op jit(solution)/shard_map/pallas_call | solution.py:316
  56.9 1.9 %shard_map.77 = (bf16[2,128,512]{2,1,0:T(8,128)(2,1)}, f32[3,64,128]{2,1,0:T(8,128)}, f32[3,256,128]{2,1,0:T(8,128)}) custom-call(bf16[2,128,512]{2,1,0:T(8,128)(2,1)} %get-tuple-element.8.enc_ref, bf16[8,128,128]{2,1,0:T(8,128)(2,1)} %get-tuple-element.9.held), custom_call_target="tpu_custom_call" | custom-call | tf_op jit(solution)/shard_map/pallas_call | solution.py:358

commit v5 on v4

--- a/solution.py
+++ b/solution.py
@@ -32,8 +32,7 @@
     clip_ref, w1_ref, w2_ref, cot_ref,
     vown, vhalo, coth, flags, flagh, uown, usend, urecv, pre, dsext,
     masks, part, send1, recv1, tiles, recv2, final,
-    sin, sva, rva, svb, rvb, svh, rvh, sct, rct, sfl, rfl, su, ru, sw, rw, sdh, rdh,
-    sa, ra, sb, rb, sc, rc, sd, rd, known,
+    sin, ra_video, sems, known,
 ):
     me = lax.axis_index("tm")
     chan = lax.axis_index("chan")
@@ -59,13 +58,12 @@
             device_id=device, device_id_type=MESH,
         )
 
-    started = []
-
-    def send(src, dst, ssem, rsem, device):
-        copy = remote(src, dst, ssem, rsem, device)
-        copy.start()
-        started.append(copy)
-        return copy
+    def arrived(semaphore, buffer):
+        pltpu.make_async_copy(buffer, buffer, semaphore).wait()
+
+    (s_video, r_behind, s_w, r_w, s_wc, r_wc, s_halo, r_halo, s_cot, r_cot, s_flag, r_flag, s_unit, r_unit,
+     s_dhalo, r_dhalo, s_a, r_a, s_b, r_b, s_c, r_c, s_d, r_d) = (sems.at[i] for i in range(24))
+    sibling = (me + 1 - 2 * lax.rem(me, 2), chan)
 
     barrier = pltpu.get_barrier_semaphore()
     near = [over_x(s) for s in range(1, NX)] + [prev, nxt, over_z(1), over_z(NZ - 1)]
@@ -98,17 +96,21 @@
 
     pl.semaphore_wait(barrier, len(near))
 
-    ahead, behind, halo = [None], [None], []
-    for s in range(1, NX):
-        ahead.append(send(video_hbm.at[2:4], vown.at[2:4, own], sva.at[s], rva.at[s], over_x(s)))
-    halo.append(send(video_hbm.at[2:4], vhalo.at[:, own], svh.at[0], rvh.at[0], nxt))
-    weights = [None]
-    for s in range(1, NX):
-        weights.append(send(w1_hbm, w1_ref.at[:, mine64], sw.at[s], rw.at[s], over_x(s)))
-    for s in range(1, NX):
-        behind.append(send(video_hbm.at[0:2], vown.at[0:2, own], svb.at[s], rvb.at[s], over_x(s)))
-    cot_copy = send(cot_hbm, coth, sct, rct, prev)
-    flag_copy = send(flags, flagh, sfl, rfl, prev)
+    for s in range(1, NX):
+        remote(video_hbm.at[2:4], vown.at[2:4, own], s_video, ra_video.at[s], over_x(s)).start()
+    remote(video_hbm.at[2:4], vhalo.at[:, own], s_halo, r_halo, nxt).start()
+    core = lax.rem(me, 2)
+    w_half = w1_hbm.at[:, block(core, 32)]
+
+    def w_place(c):
+        return w1_ref.at[:, block(2 * c + core, 32)]
+
+    for s in range(1, NX):
+        remote(w_half, w_place(chan), s_w, r_w, over_x(s)).start()
+    for s in range(1, NX):
+        remote(video_hbm.at[0:2], vown.at[0:2, own], s_video, r_behind, over_x(s)).start()
+    remote(cot_hbm, coth, s_cot, r_cot, prev).start()
+    remote(flags, flagh, s_flag, r_flag, prev).start()
 
     def greet(step, distance):
         for s in (distance, NZ - distance):
@@ -136,8 +138,8 @@
     local1 = nn(
         jnp.concatenate([w2[0], w2[1], w2[2]], axis=1), jnp.concatenate([cot[1], b, b], axis=0)
     )
-    cot_copy.wait_recv()
-    flag_copy.wait_recv()
+    arrived(r_cot, coth)
+    arrived(r_flag, flagh)
     for i in range(4):
         masks[4 + i] = coth[i // 3] * flagh[i : i + 1, :]
     e, f, g, h = (masks[4 + i] for i in range(4))
@@ -151,23 +153,25 @@
             uown[x, i] = piece
             usend[x, i] = piece.astype(BF16)
 
+    for s in range(1, NX):
+        remote(usend.at[lax.rem(chan + s, NX)], urecv.at[s], s_unit, r_unit, over_x(s)).start()
+
     pl.semaphore_wait(known.at[0], 2)
     greet(1, 2)
 
     for s in range(1, NX):
-        ahead[s].wait_recv()
         from_s = block(lax.rem(chan + NX - s, NX), 32)
-        halo.append(send(vown.at[2:4, from_s], vhalo.at[:, from_s], svh.at[s], rvh.at[s], nxt))
-    for s in range(1, NX):
-        behind[s].wait_recv()
-    sums = [None]
-    for s in range(1, NX):
-        sums.append(send(usend.at[lax.rem(chan + s, NX)], urecv.at[s], su.at[s], ru.at[s], over_x(s)))
+        arrived(ra_video.at[s], vown.at[2:4, from_s])
+        remote(vown.at[2:4, from_s], vhalo.at[:, from_s], s_halo, r_halo, nxt).start()
+    arrived(r_w, w1_ref.at[:, 0:96])
+    for s in range(1, NX):
+        part_w = w_place(lax.rem(chan + NX - s, NX))
+        remote(part_w, part_w, s_wc, r_wc, sibling).start()
     pl.semaphore_wait(known.at[1], 2)
     greet(2, 4)
 
-    for s in range(1, NX):
-        weights[s].wait_recv()
+    arrived(r_behind, vown.at[0:2, 0:96])
+    arrived(r_wc, w1_ref.at[:, 0:96])
     w1 = jnp.concatenate([w1_ref[k] for k in range(3)], axis=1)
 
     def source(t, k):
@@ -181,8 +185,7 @@
 
     for j in (1, 0):
         if j == 0:
-            for s in range(NX):
-                halo[s].wait_recv()
+            arrived(r_halo, vhalo)
         total = None
         for t in (2 * j, 2 * j + 1):
             p = nn(w1, jnp.concatenate([source(t, k) for k in range(3)], axis=0))
@@ -197,7 +200,7 @@
 
         @pl.when(s != 0)
         def _():
-            remote(send1.at[piece], recv1.at[s], sa.at[piece], ra.at[s], (z * NQ + piece, chan)).start()
+            remote(send1.at[piece], recv1.at[s], s_a, r_a, (z * NQ + piece, chan)).start()
 
     cot = [cot_ref.at[0], cot_ref.at[1]]
     a, b, c, d, e, f, g, h = (masks.at[i] for i in range(8))
@@ -216,8 +219,8 @@
             hand_over(2 * k + half)
 
     unit = uown[chan]
-    for s in range(1, NX):
-        sums[s].wait_recv()
+    arrived(r_unit, urecv.at[1:NX])
+    for s in range(1, NX):
         unit = unit + urecv[s].astype(F32)
     deltas = []
     for t in range(4):
@@ -231,12 +234,12 @@
     part[7, 64:128, :] = jnp.zeros((64, 128), F32)
     hand_over(6)
     hand_over(7)
-    dhalo = send(dsext.at[2:4], dsext.at[0:2], sdh, rdh, nxt)
+    remote(dsext.at[2:4], dsext.at[0:2], s_dhalo, r_dhalo, nxt).start()
     pl.semaphore_wait(known.at[2], 2)
 
     total = part[q]
+    arrived(r_a, recv1.at[1:NQ])
     for s in range(1, NQ):
-        remote(send1.at[0], recv1.at[s], sa.at[0], ra.at[s], in_z(s)).wait_recv()
         total = total + recv1[s].astype(F32)
     tiles[...] = total.astype(BF16).reshape(8, 16, 128)
 
@@ -247,10 +250,10 @@
         return lax.rem(z + s, NZ) // 2
 
     def to_owner(s):
-        return remote(tiles.at[tile_of(s)], recv2.at[s], sb.at[s], rb.at[s], over_z(s))
+        return remote(tiles.at[tile_of(s)], recv2.at[s], s_b, r_b, over_z(s))
 
     def from_owner(s):
-        return remote(final.at[mine], final.at[mine], sc.at[s], rc.at[s], over_z(s))
+        return remote(final.at[mine], final.at[mine], s_c, r_c, over_z(s))
 
     @pl.when(owner)
     def _():
@@ -262,7 +265,7 @@
         for s in range(1, NZ, 2):
             to_owner(s).start()
 
-    dhalo.wait_recv()
+    arrived(r_dhalo, dsext.at[0:2])
     w2t = jnp.concatenate([w2_ref[k] for k in range(3)], axis=0)
     for j in range(2):
         sources = [dsext[jnp.maximum(j - k, start2[j]) + 2] for k in range(3)]
@@ -270,43 +273,53 @@
 
     @pl.when(owner)
     def _():
+        arrived(r_b, recv2.at[1:NZ])
         total = tiles[mine].astype(F32)
         for s in range(1, NZ):
-            to_owner(s).wait_recv()
             total = total + recv2[s].astype(F32)
         final[mine] = total.astype(BF16)
         for s in range(1, NZ):
             from_owner(s).start()
-        for s in range(2, NZ, 2):
-            from_owner(s).wait_recv()
-            to_owner(s).wait_send()
-        for s in range(1, NZ):
-            from_owner(s).wait_send()
+        arrived(r_c, recv2.at[0:7])
+        arrived(s_b, recv2.at[0:7])
+        arrived(s_c, recv2.at[1:NZ])
 
     @pl.when(jnp.logical_not(owner))
     def _():
-        for s in range(1, NZ, 2):
-            from_owner(s).wait_recv()
-            to_owner(s).wait_send()
+        arrived(r_c, recv2.at[0:8])
+        arrived(s_b, recv2.at[0:8])
 
     held[q] = final[...].reshape(128, 128)
-    fourth = [send(held.at[q], held.at[q], sd.at[s], rd.at[s], in_z(s)) for s in range(1, NQ)]
-    for piece in range(NQ):
-        @pl.when(piece != q)
-        def _():
-            remote(send1.at[piece], recv1.at[1], sa.at[piece], ra.at[1], nxt).wait_send()
-    for copy in fourth:
-        copy.wait_recv()
-    for copy in started:
-        copy.wait_send()
-
-
-def write_kernel(enc_ref, held, out_ref, o1_ref, o2_ref):
-    out_ref[...] = enc_ref[...]
+    for s in range(1, NQ):
+        remote(held.at[q], held.at[q], s_d, r_d, in_z(s)).start()
+    arrived(s_video, usend.at[0:3])
+    arrived(s_w, w1_ref.at[:, 0:96])
+    arrived(s_wc, w1_ref.at[:, 0:96])
+    arrived(s_halo, vhalo)
+    arrived(s_cot, coth)
+    arrived(s_flag, flagh)
+    arrived(s_unit, usend.at[0:3])
+    arrived(s_dhalo, dsext.at[0:2])
+    arrived(s_a, recv1.at[1:NQ])
+    arrived(r_d, held.at[1:NQ])
+    arrived(s_d, held.at[1:NQ])
+
+
+def write_kernel(enc_ref, held, out_hbm, o1_hbm, o2_hbm, o1_ref, o2_ref, sems):
+    copies = [
+        pltpu.make_async_copy(src, dst, sems.at[i])
+        for i, (src, dst) in enumerate([(enc_ref, out_hbm), (o1_ref, o1_hbm), (o2_ref, o2_hbm)])
+    ]
+    copies[0].start()
     for k in range(3):
         o2_ref[k] = held[2 * k : 2 * k + 2].reshape(256, 128).astype(F32) * (131072.0 ** -0.5)
+    copies[2].start()
+    for k in range(3):
         piece = held[6 + k // 2, (k % 2) * 64 : (k % 2) * 64 + 64, :]
         o1_ref[k] = piece.astype(F32) * (262144.0 ** -0.5)
+    copies[1].start()
+    for copy in copies:
+        copy.wait()
 
 
 def per_device(video, clip_start, first_conv_weight, second_conv_weight, cotangent):
@@ -344,17 +357,17 @@
             pltpu.VMEM((NZ, 16, 128), BF16),
             pltpu.VMEM((8, 16, 128), BF16),
             dma((5,)),
-        ]
-        + [dma((NX,))] * 6
-        + [dma(())] * 4
-        + [dma((NX,))] * 4
-        + [dma(())] * 2
-        + [dma((NQ,)), dma((NQ,)), dma((NZ,)), dma((NZ,)), dma((NZ,)), dma((NZ,)), dma((NQ,)), dma((NQ,))]
-        + [pltpu.SemaphoreType.REGULAR((3,))],
+            dma((NX,)),
+            dma((24,)),
+            pltpu.SemaphoreType.REGULAR((3,)),
+        ],
         compiler_params=pltpu.CompilerParams(
-            collective_id=0, has_side_effects=True, vmem_limit_bytes=62 * 1024 * 1024
+            collective_id=0, has_side_effects=True, vmem_limit_bytes=40 * 1024 * 1024
         ),
-    )(clip_start, video, first_conv_weight.transpose(0, 2, 1), second_conv_weight, cotangent)
+    )(*(
+        pltpu.with_memory_space_constraint(x, pltpu.HBM)
+        for x in (clip_start, video, first_conv_weight.transpose(0, 2, 1), second_conv_weight, cotangent)
+    ))
     encoded, first_grad, second_grad = pl.pallas_call(
         write_kernel,
         out_shape=(
@@ -363,8 +376,10 @@
             jax.ShapeDtypeStruct((3, 256, 128), F32),
         ),
         in_specs=[vmem] * 2,
-        out_specs=(vmem,) * 3,
-    )(encoded, held)
+        out_specs=(hbm,) * 3,
+        scratch_shapes=[pltpu.VMEM((3, 64, 128), F32), pltpu.VMEM((3, 256, 128), F32), dma((3,))],
+        compiler_params=pltpu.CompilerParams(vmem_limit_bytes=8 * 1024 * 1024),
+    )(*(pltpu.with_memory_space_constraint(x, pltpu.VMEM) for x in (encoded, held)))
     return encoded, first_grad.transpose(0, 2, 1), second_grad
 
 

time: 59 us -> 54.7 us (0.927)
  Pallas kernels: 58.2 us -> 53.9 us
    pallas_call x1, Pallas kernels: 56.3 us -> 53.1 us  [per_device(): pl.pallas_call(kernel, out_shape=(jax.ShapeDtypeStruct((2, 128, 512), BF1...]
    pallas_call x1, Pallas kernels: 1.91 us -> 0.89 us  [per_device(): pl.pallas_call(write_kernel, out_shape=(jax.ShapeDtypeStruct((2, 128, 512...]
where the time goes in v5:
time: 54.7 us; the launch traced here: 54.6 us
  Pallas kernels  53.9 us (99%)
  between operations  0.64 us (1%)
    pallas_call x1, Pallas kernels, per_device(): pl.pallas_call(kernel, out_shape=(jax.ShapeDtypeStruct((2, 128, 512), BF1...  53.1 us

profile of v5, /device:TPU:1, one launch (start us, length us, event | category | flops | bytes accessed | tf_op | source)
XLA Modules:
  0.0 54.6 jit_solution(16656603153590504083)
XLA Ops:
  0.6 53.1 %shard_map.76 = (bf16[2,128,512]{2,1,0:T(8,128)(2,1)S(1)}, bf16[8,128,128]{2,1,0:T(8,128)(2,1)S(1)}) custom-call(s32[4]{0:T(128)} %clip_hbm.1, bf16[4,32,512]{2,1,0:T(8,128)(2,1)} %video_hbm.1, bf16[3,64,128]{2,1,0:T(8,128)(2,1)} %bitcast.2, bf16[3,256,128]{2,1,0:T(8,128)(2,1)} %w2_hbm.1, bf16[2,128,512]{2,1,0:T(8,128)(2,1)} %cot_hbm.1), custom_call_target="tpu_custom_call" | custom-call | tf_op jit(solution)/shard_map/pallas_call | solution.py:329
  53.7 0.9 %shard_map.77 = (bf16[2,128,512]{2,1,0:T(8,128)(2,1)}, f32[3,64,128]{2,1,0:T(8,128)}, f32[3,256,128]{2,1,0:T(8,128)}) custom-call(bf16[2,128,512]{2,1,0:T(8,128)(2,1)S(1)} %get-tuple-element.8.enc_ref, bf16[8,128,128]{2,1,0:T(8,128)(2,1)S(1)} %get-tuple-element.9.held), custom_call_target="tpu_custom_call" | custom-call | tf_op jit(solution)/shard_map/pallas_call | solution.py:371

commit v6 on v5

--- a/solution.py
+++ b/solution.py
@@ -66,10 +66,18 @@
     sibling = (me + 1 - 2 * lax.rem(me, 2), chan)
 
     barrier = pltpu.get_barrier_semaphore()
-    near = [over_x(s) for s in range(1, NX)] + [prev, nxt, over_z(1), over_z(NZ - 1)]
+    near = [over_x(s) for s in range(1, NX)] + [over_z(1), over_z(NZ - 1)]
     near += [in_z(s) for s in range(1, NQ)]
     for device in near:
         pl.semaphore_signal(barrier, inc=1, device_id=device, device_id_type=MESH)
+
+    @pl.when(q == 0)
+    def _():
+        pl.semaphore_signal(barrier, inc=1, device_id=prev, device_id_type=MESH)
+
+    @pl.when(q == NQ - 1)
+    def _():
+        pl.semaphore_signal(barrier, inc=1, device_id=nxt, device_id_type=MESH)
 
     own, mine64 = block(chan, 32), block(chan, 64)
     fetch = [
@@ -94,9 +102,9 @@
         [jnp.full((1, 512), flag(r), F32) for r in rows] + [jnp.zeros((12, 512), F32)], axis=0
     ).astype(BF16)
 
-    pl.semaphore_wait(barrier, len(near))
-
-    for s in range(1, NX):
+    pl.semaphore_wait(barrier, len(near) + 1 - (lax.rem(q, NQ - 1) + NQ - 3) // (NQ - 2))
+
+    for s in (2, 1, 3):
         remote(video_hbm.at[2:4], vown.at[2:4, own], s_video, ra_video.at[s], over_x(s)).start()
     remote(video_hbm.at[2:4], vhalo.at[:, own], s_halo, r_halo, nxt).start()
     core = lax.rem(me, 2)
@@ -105,9 +113,9 @@
     def w_place(c):
         return w1_ref.at[:, block(2 * c + core, 32)]
 
-    for s in range(1, NX):
+    for s in (2, 1, 3):
         remote(w_half, w_place(chan), s_w, r_w, over_x(s)).start()
-    for s in range(1, NX):
+    for s in (2, 1, 3):
         remote(video_hbm.at[0:2], vown.at[0:2, own], s_video, r_behind, over_x(s)).start()
     remote(cot_hbm, coth, s_cot, r_cot, prev).start()
     remote(flags, flagh, s_flag, r_flag, prev).start()
@@ -153,7 +161,7 @@
             uown[x, i] = piece
             usend[x, i] = piece.astype(BF16)
 
-    for s in range(1, NX):
+    for s in (2, 1, 3):
         remote(usend.at[lax.rem(chan + s, NX)], urecv.at[s], s_unit, r_unit, over_x(s)).start()
 
     pl.semaphore_wait(known.at[0], 2)
@@ -190,7 +198,8 @@
         for t in (2 * j, 2 * j + 1):
             p = nn(w1, jnp.concatenate([source(t, k) for k in range(3)], axis=0))
             pre[t] = p
-            act = p * jax.nn.sigmoid(p)
+            h = 0.5 * p
+            act = h + h * jnp.tanh(h)
             total = act if total is None else total + act
         dsext[2 + j] = (0.5 * total).astype(BF16)
 
@@ -204,18 +213,20 @@
 
     cot = [cot_ref.at[0], cot_ref.at[1]]
     a, b, c, d, e, f, g, h = (masks.at[i] for i in range(8))
-    terms = [
-        [(0, cot[0]), (1, cot[1])],
-        [(0, a), (1, b), (0, c), (1, e)],
-        [(0, a), (1, b), (0, d), (1, f), (0, g), (1, h)],
-    ]
+    def stacked(*refs):
+        return jnp.concatenate([r[...] for r in refs], axis=0)
 
     @pl.loop(0, 2)
     def _(half):
+        down0 = dsext[2, block(half, 128), :]
+        down1 = dsext[3, block(half, 128), :]
+        same = nt(down0, stacked(cot[0], a)) + nt(down1, stacked(cot[1], b))
+        later = nt(down0, stacked(c, d)) + nt(down1, stacked(e, f))
+        last = nt(down0, g[...]) + nt(down1, h[...])
+        part[half] = same[:, :128]
+        part[2 + half] = same[:, 128:] + later[:, :128]
+        part[4 + half] = same[:, 128:] + later[:, 128:] + last
         for k in range(3):
-            right = jnp.concatenate([v[...] for _, v in terms[k]], axis=1)
-            left = [dsext[2 + i, block(half, 128), :] for i, _ in terms[k]]
-            part[2 * k + half] = nt(jnp.concatenate(left, axis=1), right)
             hand_over(2 * k + half)
 
     unit = uown[chan]
@@ -257,12 +268,12 @@
 
     @pl.when(owner)
     def _():
-        for s in range(2, NZ, 2):
+        for s in (8, 6, 10, 4, 12, 2, 14):
             to_owner(s).start()
 
     @pl.when(jnp.logical_not(owner))
     def _():
-        for s in range(1, NZ, 2):
+        for s in (7, 9, 5, 11, 3, 13, 1, 15):
             to_owner(s).start()
 
     arrived(r_dhalo, dsext.at[0:2])
@@ -278,7 +289,7 @@
         for s in range(1, NZ):
             total = total + recv2[s].astype(F32)
         final[mine] = total.astype(BF16)
-        for s in range(1, NZ):
+        for s in (8, 7, 9, 6, 10, 5, 11, 4, 12, 3, 13, 2, 14, 1, 15):
             from_owner(s).start()
         arrived(r_c, recv2.at[0:7])
         arrived(s_b, recv2.at[0:7])
@@ -290,7 +301,7 @@
         arrived(s_b, recv2.at[0:8])
 
     held[q] = final[...].reshape(128, 128)
-    for s in range(1, NQ):
+    for s in (4, 3, 5, 2, 6, 1, 7):
         remote(held.at[q], held.at[q], s_d, r_d, in_z(s)).start()
     arrived(s_video, usend.at[0:3])
     arrived(s_w, w1_ref.at[:, 0:96])

time: 54.7 us -> 53.1 us (0.971)
  Pallas kernels: 53.9 us -> 52.3 us
    pallas_call x1, Pallas kernels: 53.1 us -> 51.4 us  [per_device(): pl.pallas_call(kernel, out_shape=(jax.ShapeDtypeStruct((2, 128, 512), BF1...]
where the time goes in v6:
time: 53.1 us; the launch traced here: 52.9 us
  Pallas kernels  52.3 us (98%)
  between operations  0.64 us (1%)
    pallas_call x1, Pallas kernels, per_device(): pl.pallas_call(kernel, out_shape=(jax.ShapeDtypeStruct((2, 128, 512), BF1...  51.4 us

profile of v6, /device:TPU:1, one launch (start us, length us, event | category | flops | bytes accessed | tf_op | source)
XLA Modules:
  0.0 52.9 jit_solution(1413535491490074289)
XLA Ops:
  0.6 51.4 %shard_map.76 = (bf16[2,128,512]{2,1,0:T(8,128)(2,1)S(1)}, bf16[8,128,128]{2,1,0:T(8,128)(2,1)S(1)}) custom-call(s32[4]{0:T(128)} %clip_hbm.1, bf16[4,32,512]{2,1,0:T(8,128)(2,1)} %video_hbm.1, bf16[3,64,128]{2,1,0:T(8,128)(2,1)} %bitcast.2, bf16[3,256,128]{2,1,0:T(8,128)(2,1)} %w2_hbm.1, bf16[2,128,512]{2,1,0:T(8,128)(2,1)} %cot_hbm.1), custom_call_target="tpu_custom_call" | custom-call | tf_op jit(solution)/shard_map/pallas_call | solution.py:340
  52.1 0.9 %shard_map.77 = (bf16[2,128,512]{2,1,0:T(8,128)(2,1)}, f32[3,64,128]{2,1,0:T(8,128)}, f32[3,256,128]{2,1,0:T(8,128)}) custom-call(bf16[2,128,512]{2,1,0:T(8,128)(2,1)S(1)} %get-tuple-element.8.enc_ref, bf16[8,128,128]{2,1,0:T(8,128)(2,1)S(1)} %get-tuple-element.9.held), custom_call_target="tpu_custom_call" | custom-call | tf_op jit(solution)/shard_map/pallas_call | solution.py:382

commit v7 on v6

--- a/solution.py
+++ b/solution.py
@@ -31,8 +31,8 @@
     enc_ref, held,
     clip_ref, w1_ref, w2_ref, cot_ref,
     vown, vhalo, coth, flags, flagh, uown, usend, urecv, pre, dsext,
-    masks, part, send1, recv1, tiles, recv2, final,
-    sin, ra_video, sems, known,
+    masks, part, send1, recv1, tiles, recv2,
+    sin, ra_video, r_c, sems, known,
 ):
     me = lax.axis_index("tm")
     chan = lax.axis_index("chan")
@@ -62,7 +62,7 @@
         pltpu.make_async_copy(buffer, buffer, semaphore).wait()
 
     (s_video, r_behind, s_w, r_w, s_wc, r_wc, s_halo, r_halo, s_cot, r_cot, s_flag, r_flag, s_unit, r_unit,
-     s_dhalo, r_dhalo, s_a, r_a, s_b, r_b, s_c, r_c, s_d, r_d) = (sems.at[i] for i in range(24))
+     s_dhalo, r_dhalo, s_a, r_a, s_b, r_b, s_c, s_d, r_d) = (sems.at[i] for i in range(23))
     sibling = (me + 1 - 2 * lax.rem(me, 2), chan)
 
     barrier = pltpu.get_barrier_semaphore()
@@ -263,8 +263,16 @@
     def to_owner(s):
         return remote(tiles.at[tile_of(s)], recv2.at[s], s_b, r_b, over_z(s))
 
+    def slot_at(there):
+        return lax.rem(mine + 10 - (there + 1) // 2, 8)
+
     def from_owner(s):
-        return remote(final.at[mine], final.at[mine], s_c, r_c, over_z(s))
+        slot = slot_at(lax.rem(z + s, NZ))
+        return remote(held.at[q, slot_at(z)], held.at[q, slot], s_c, r_c.at[slot // 4], over_z(s))
+
+    def spread(part_of):
+        for s in (4, 3, 5, 2, 6, 1, 7):
+            remote(held.at[q, part_of], held.at[q, part_of], s_d, r_d, in_z(s)).start()
 
     @pl.when(owner)
     def _():
@@ -288,21 +296,25 @@
         total = tiles[mine].astype(F32)
         for s in range(1, NZ):
             total = total + recv2[s].astype(F32)
-        final[mine] = total.astype(BF16)
+        held[q, slot_at(z)] = total.astype(BF16)
         for s in (8, 7, 9, 6, 10, 5, 11, 4, 12, 3, 13, 2, 14, 1, 15):
             from_owner(s).start()
-        arrived(r_c, recv2.at[0:7])
+        arrived(r_c.at[0], recv2.at[0:3])
         arrived(s_b, recv2.at[0:7])
+
+    @pl.when(jnp.logical_not(owner))
+    def _():
+        arrived(r_c.at[0], recv2.at[0:4])
+        arrived(s_b, recv2.at[0:8])
+
+    spread(pl.ds(0, 4))
+    arrived(r_c.at[1], recv2.at[0:4])
+    spread(pl.ds(4, 4))
+
+    @pl.when(owner)
+    def _():
         arrived(s_c, recv2.at[1:NZ])
 
-    @pl.when(jnp.logical_not(owner))
-    def _():
-        arrived(r_c, recv2.at[0:8])
-        arrived(s_b, recv2.at[0:8])
-
-    held[q] = final[...].reshape(128, 128)
-    for s in (4, 3, 5, 2, 6, 1, 7):
-        remote(held.at[q], held.at[q], s_d, r_d, in_z(s)).start()
     arrived(s_video, usend.at[0:3])
     arrived(s_w, w1_ref.at[:, 0:96])
     arrived(s_wc, w1_ref.at[:, 0:96])
@@ -322,12 +334,20 @@
         for i, (src, dst) in enumerate([(enc_ref, out_hbm), (o1_ref, o1_hbm), (o2_ref, o2_hbm)])
     ]
     copies[0].start()
-    for k in range(3):
-        o2_ref[k] = held[2 * k : 2 * k + 2].reshape(256, 128).astype(F32) * (131072.0 ** -0.5)
+    shift = 10 - (lax.axis_index("tm") // NQ + 1) // 2
+
+    def tile(piece, i):
+        return held[piece, lax.rem(i + shift, 8)].astype(F32)
+
+    for piece in range(6):
+        for i in range(8):
+            rows = slice(128 * (piece % 2) + 16 * i, 128 * (piece % 2) + 16 * i + 16)
+            o2_ref[piece // 2, rows, :] = tile(piece, i) * (131072.0 ** -0.5)
     copies[2].start()
     for k in range(3):
-        piece = held[6 + k // 2, (k % 2) * 64 : (k % 2) * 64 + 64, :]
-        o1_ref[k] = piece.astype(F32) * (262144.0 ** -0.5)
+        for i in range(4):
+            part = tile(6 + k // 2, 4 * (k % 2) + i)
+            o1_ref[k, 16 * i : 16 * i + 16, :] = part * (262144.0 ** -0.5)
     copies[1].start()
     for copy in copies:
         copy.wait()
@@ -341,7 +361,7 @@
         kernel,
         out_shape=(
             jax.ShapeDtypeStruct((2, 128, 512), BF16),
-            jax.ShapeDtypeStruct((NQ, 128, 128), BF16),
+            jax.ShapeDtypeStruct((NQ, 8, 16, 128), BF16),
         ),
         in_specs=[hbm] * 5,
         out_specs=(vmem, vmem),
@@ -366,10 +386,10 @@
             pltpu.VMEM((NQ, 128, 128), BF16),
             pltpu.VMEM((8, 16, 128), BF16),
             pltpu.VMEM((NZ, 16, 128), BF16),
-            pltpu.VMEM((8, 16, 128), BF16),
             dma((5,)),
             dma((NX,)),
-            dma((24,)),
+            dma((2,)),
+            dma((23,)),
             pltpu.SemaphoreType.REGULAR((3,)),
         ],
         compiler_params=pltpu.CompilerParams(

time: 53.1 us -> 52.5 us (0.989)
  no operation moved by 1% of the time
where the time goes in v7:
time: 52.5 us; the launch traced here: 52.4 us
  Pallas kernels  51.8 us (99%)
  between operations  0.64 us (1%)
    pallas_call x1, Pallas kernels, per_device(): pl.pallas_call(kernel, out_shape=(jax.ShapeDtypeStruct((2, 128, 512), BF1...  50.9 us

profile of v7, /device:TPU:1, one launch (start us, length us, event | category | flops | bytes accessed | tf_op | source)
XLA Modules:
  0.0 52.4 jit_solution(11653618413865261927)
XLA Ops:
  0.6 50.9 %shard_map.76 = (bf16[2,128,512]{2,1,0:T(8,128)(2,1)S(1)}, bf16[8,8,16,128]{3,2,1,0:T(8,128)(2,1)S(1)}) custom-call(s32[4]{0:T(128)} %clip_hbm.1, bf16[4,32,512]{2,1,0:T(8,128)(2,1)} %video_hbm.1, bf16[3,64,128]{2,1,0:T(8,128)(2,1)} %bitcast.2, bf16[3,256,128]{2,1,0:T(8,128)(2,1)} %w2_hbm.1, bf16[2,128,512]{2,1,0:T(8,128)(2,1)} %cot_hbm.1), custom_call_target="tpu_custom_call" | custom-call | tf_op jit(solution)/shard_map/pallas_call | solution.py:360
  51.5 0.9 %shard_map.77 = (bf16[2,128,512]{2,1,0:T(8,128)(2,1)}, f32[3,64,128]{2,1,0:T(8,128)}, f32[3,256,128]{2,1,0:T(8,128)}) custom-call(bf16[2,128,512]{2,1,0:T(8,128)(2,1)S(1)} %get-tuple-element.8.enc_ref, bf16[8,8,16,128]{3,2,1,0:T(8,128)(2,1)S(1)} %get-tuple-element.9.held), custom_call_target="tpu_custom_call" | custom-call | tf_op jit(solution)/shard_map/pallas_call | solution.py:402

commit v8 on v7

--- a/solution.py
+++ b/solution.py
@@ -284,12 +284,6 @@
         for s in (7, 9, 5, 11, 3, 13, 1, 15):
             to_owner(s).start()
 
-    arrived(r_dhalo, dsext.at[0:2])
-    w2t = jnp.concatenate([w2_ref[k] for k in range(3)], axis=0)
-    for j in range(2):
-        sources = [dsext[jnp.maximum(j - k, start2[j]) + 2] for k in range(3)]
-        enc_ref[j] = tn(w2t, jnp.concatenate(sources, axis=0)).astype(BF16)
-
     @pl.when(owner)
     def _():
         arrived(r_b, recv2.at[1:NZ])
@@ -299,6 +293,15 @@
         held[q, slot_at(z)] = total.astype(BF16)
         for s in (8, 7, 9, 6, 10, 5, 11, 4, 12, 3, 13, 2, 14, 1, 15):
             from_owner(s).start()
+
+    arrived(r_dhalo, dsext.at[0:2])
+    w2t = jnp.concatenate([w2_ref[k] for k in range(3)], axis=0)
+    for j in range(2):
+        sources = [dsext[jnp.maximum(j - k, start2[j]) + 2] for k in range(3)]
+        enc_ref[j] = tn(w2t, jnp.concatenate(sources, axis=0)).astype(BF16)
+
+    @pl.when(owner)
+    def _():
         arrived(r_c.at[0], recv2.at[0:3])
         arrived(s_b, recv2.at[0:7])
 

time: 52.5 us -> 52.5 us (level)
  no operation moved by 1% of the time
where the time goes in v8:
time: 52.5 us; the launch traced here: 52.4 us
  Pallas kernels  51.8 us (99%)
  between operations  0.64 us (1%)
    pallas_call x1, Pallas kernels, per_device(): pl.pallas_call(kernel, out_shape=(jax.ShapeDtypeStruct((2, 128, 512), BF1...  50.9 us

profile of v8, /device:TPU:1, one launch (start us, length us, event | category | flops | bytes accessed | tf_op | source)
XLA Modules:
  0.0 52.4 jit_solution(10662528094676574844)
XLA Ops:
  0.6 50.9 %shard_map.76 = (bf16[2,128,512]{2,1,0:T(8,128)(2,1)S(1)}, bf16[8,8,16,128]{3,2,1,0:T(8,128)(2,1)S(1)}) custom-call(s32[4]{0:T(128)} %clip_hbm.1, bf16[4,32,512]{2,1,0:T(8,128)(2,1)} %video_hbm.1, bf16[3,64,128]{2,1,0:T(8,128)(2,1)} %bitcast.2, bf16[3,256,128]{2,1,0:T(8,128)(2,1)} %w2_hbm.1, bf16[2,128,512]{2,1,0:T(8,128)(2,1)} %cot_hbm.1), custom_call_target="tpu_custom_call" | custom-call | tf_op jit(solution)/shard_map/pallas_call | solution.py:363
  51.5 0.9 %shard_map.77 = (bf16[2,128,512]{2,1,0:T(8,128)(2,1)}, f32[3,64,128]{2,1,0:T(8,128)}, f32[3,256,128]{2,1,0:T(8,128)}) custom-call(bf16[2,128,512]{2,1,0:T(8,128)(2,1)S(1)} %get-tuple-element.8.enc_ref, bf16[8,8,16,128]{3,2,1,0:T(8,128)(2,1)S(1)} %get-tuple-element.9.held), custom_call_target="tpu_custom_call" | custom-call | tf_op jit(solution)/shard_map/pallas_call | solution.py:405
